TPU v7x, 32 devices: a whole 2x2x4 slice. The times are simulated.
32 devices in a mesh: seq: 8 (over y, x, core), kv: 4 (over z).
Axes of the slice: x: 2, y: 2, z: 4, core: 2. Of those that a mesh axis runs over, the one named last changes fastest.
Arguments:
- activations: bfloat16 [2, 2048, 2048], P(None, 'seq'), may hold values from -6 to 6
- cotangent: bfloat16 [2, 2048, 2048], P(None, 'seq'), may hold values from -6 to 6
- document_starts: int32 [2, 4], replicated, may hold values from 0 to 2048, as said below
- norm_gain_pair: bfloat16 [2, 2048], P(None, 'seq'), may hold values from 0.5 to 1.5
- query_projection_weight: bfloat16 [2048, 2048], P('seq', 'kv'), may hold values from -0.125 to 0.125
- key_value_weight: bfloat16 [2, 2048, 512], P(None, 'seq', 'kv'), may hold values from -0.125 to 0.125
- output_projection_weight: bfloat16 [2048, 2048], P('kv', 'seq'), may hold values from -0.5 to 0.5
- gate_up_weight: bfloat16 [2, 2048, 8192], P(None, 'seq', 'kv'), may hold values from -0.125 to 0.125
- down_weight: bfloat16 [8192, 2048], P('kv', 'seq'), may hold values from -0.0625 to 0.0625
- adapter_down_maps: bfloat16 [2048, 24], P('seq'), may hold values from -0.125 to 0.125
- query_adapter_up: bfloat16 [8, 2048], P(None, 'kv'), may hold values from -1 to 1
- keyval_adapter_up: bfloat16 [2, 8, 512], P(None, None, 'kv'), may hold values from -1 to 1
- output_adapter_down: bfloat16 [2048, 8], P('kv'), may hold values from -1 to 1
- output_adapter_up: bfloat16 [8, 2048], P(None, 'seq'), may hold values from -2 to 2
- hedgehog_maps: float32 [2, 32, 64, 64], P(None, 'kv'), may hold values from -0.75 to 0.75
Outputs:
- block_out: bfloat16 [2, 2048, 2048], P(None, 'seq', 'kv')
- grad_input: float32 [2, 2048, 2048], P(None, 'seq')
- grad_gains: float32 [2, 2048], P(None, 'seq')
- grad_query: float32 [2048, 2048], P('seq', 'kv')
- grad_keyval: float32 [2, 2048, 512], P(None, 'seq', 'kv')
- grad_project: float32 [2048, 2048], P('kv', 'seq')
- grad_gateup: float32 [2, 2048, 8192], P(None, 'seq', 'kv')
- grad_down: float32 [8192, 2048], P('kv', 'seq')
- grad_enter: float32 [2048, 24], P('seq')
- grad_lora_query: float32 [8, 2048], P(None, 'kv')
- grad_lora_keyval: float32 [2, 8, 512], P(None, None, 'kv')
- grad_reduce: float32 [2048, 8], P('kv')
- grad_expand: float32 [8, 2048], P(None, 'seq')
- grad_maps: float32 [2, 32, 64, 64], P(None, 'kv')
Inputs may be any that keep to these rules, and one draw needn't show every extreme that they name: `document_starts`: each row never falls and begins with 0; an entry equal to 2048 opens an empty document at the end. In one micro-batch, drawn from the seed, the row is 0 followed by 2048 only: one document spans all its tokens. Every document that is not empty has 1024 tokens or more.
All inputs are finite; a program needn't handle non-finite values.
Results may differ from a plain program's by a relative error of at most 0.02.
Values may be sent and summed in bfloat16 or wider, within the bound.
No kernel may reach another device: no remote copies, remote signals or barrier semaphores. Data moves between devices by JAX's collectives and lax.ppermute only.
A program may use at most 384 MiB of HBM per device.

v0:
```python
import jax
import jax.numpy as jnp
from jax import lax
from jax.sharding import PartitionSpec as P

MODEL_WIDTH = 2048
QUERY_HEADS = 32
KEY_HEADS = 8
HEAD_SIZE = 64
ADAPTER_RANK = 8
WIN = 64
MB = 2


EPSILON = 1e-05
EXACT_MODE = lax.Precision.HIGHEST


def passed_along(value, axis, steps):
    count = lax.axis_size(axis)
    leading, last = (max(0, -steps), min(count, count - steps))
    return lax.ppermute(value, axis, [(source, source + steps) for source in range(leading, last)])


def prefix(value, axis, combine, identity):
    count, position = (lax.axis_size(axis), lax.axis_index(axis))
    everything = jax.tree.map(
        lambda part, kind: lax.all_gather(part.astype(kind), axis),
        value,
        (jnp.bfloat16, jnp.bfloat16, jnp.bfloat16),
    )
    start = jax.tree.map(
        lambda part, zero: jnp.broadcast_to(jnp.asarray(zero, part.dtype), part.shape),
        value,
        identity,
    )

    def turn(k, before):
        reached = k < position
        new = combine(
            before, jax.tree.map(lambda part, own: part[k].astype(own.dtype), everything, value)
        )
        return jax.tree.map(lambda a, b: jnp.where(reached, a, b), new, before)

    return lax.fori_loop(0, count, turn, start)


def prefix_2(value, axis, combine, identity):
    count, position = (lax.axis_size(axis), lax.axis_index(axis))
    everything = jax.tree.map(
        lambda part, kind: lax.all_gather(part.astype(kind), axis),
        value,
        jax.tree.map(lambda a: jnp.bfloat16 if a.dtype == jnp.float32 else a.dtype, value),
    )
    start = jax.tree.map(
        lambda part, zero: jnp.broadcast_to(jnp.asarray(zero, part.dtype), part.shape),
        value,
        identity,
    )

    def turn(k, before):
        at = count - 1 - k
        reached = at > position
        new = combine(
            before, jax.tree.map(lambda part, own: part[at].astype(own.dtype), everything, value)
        )
        return jax.tree.map(lambda a, b: jnp.where(reached, a, b), new, before)

    return lax.fori_loop(0, count, turn, start)


def low(v):
    rounded = lax.optimization_barrier(v.astype(jnp.bfloat16)).astype(jnp.float32)
    return v + lax.stop_gradient(rounded - v)


def product_value(left, right):
    return jnp.dot(left, right, preferred_element_type=jnp.float32)


def doc_of(starts, positions):
    counted = jnp.sum(
        (starts[None, :] <= positions[:, None]).astype(jnp.int32), axis=1, dtype=jnp.int32
    )
    return counted - 1


def feature(values, maps):
    projected = jnp.einsum("rhd,hde->rhe", values, maps, precision=EXACT_MODE)
    return jnp.concatenate(
        [jax.nn.softmax(projected, axis=-1), jax.nn.softmax(-projected, axis=-1)], axis=-1
    )


def rms_scale(values):
    return lax.rsqrt(jnp.mean(values * values, axis=-1, keepdims=True) + EPSILON)


def mix_states(earlier, later):
    return (
        later[2] * earlier[0] + later[0],
        later[2] * earlier[1] + later[1],
        earlier[2] * later[2],
    )


def key_side(key_ext, maps_key):
    repeated = jnp.repeat(key_ext, QUERY_HEADS // KEY_HEADS, axis=1)
    return (repeated, feature(repeated, maps_key))


def state_terms(feat_range, value_range, keep_mask):
    value_repeated = jnp.repeat(value_range, QUERY_HEADS // KEY_HEADS, axis=1)
    masked_scores = feat_range * keep_mask[:, None, None]
    return (
        jnp.einsum("pae,pat->aet", masked_scores, value_repeated, precision=EXACT_MODE),
        jnp.sum(masked_scores, axis=0),
    )


def attend(
    query_in,
    key_rep,
    value_ext,
    maps_query,
    feature_key,
    previous_state,
    norm_prev,
    near_mask,
    distant_mask,
    use_state,
):
    value_repeated = jnp.repeat(value_ext, QUERY_HEADS // KEY_HEADS, axis=1)
    scores = jnp.einsum("qhd,khd->hqk", query_in, key_rep, precision=EXACT_MODE) * HEAD_SIZE ** (
        -0.5
    )
    expo_terms = jnp.where(near_mask[None], jnp.exp(scores), 0.0)
    feature_query = feature(query_in, maps_query)
    linear_parts = jnp.where(
        distant_mask[None],
        jnp.einsum("ain,pin->iap", feature_query, feature_key, precision=EXACT_MODE),
        0.0,
    )
    numerator = (
        jnp.einsum("hqk,khd->qhd", low(expo_terms), value_repeated, precision=EXACT_MODE)
        + jnp.einsum("hqk,khd->qhd", linear_parts, value_repeated, precision=EXACT_MODE)
        + use_state[:, None, None]
        * jnp.einsum("qhf,hfd->qhd", feature_query, previous_state, precision=EXACT_MODE)
    )
    denominator = (
        jnp.sum(expo_terms, axis=-1)
        + jnp.sum(linear_parts, axis=-1)
        + use_state[None, :]
        * jnp.einsum("qhf,hf->hq", feature_query, norm_prev, precision=EXACT_MODE)
    )
    return numerator / jnp.transpose(denominator)[:, :, None]


def add_trees(total, extra):
    if total is None:
        return extra
    return jax.tree.map(jnp.add, total, extra)


def per_device(
    activations,
    cotangent,
    document_starts,
    norm_gain_pair,
    query_projection_weight,
    key_value_weight,
    output_projection_weight,
    gate_up_weight,
    down_weight,
    adapter_down_maps,
    query_adapter_up,
    keyval_adapter_up,
    output_adapter_down,
    output_adapter_up,
    hedgehog_maps,
):
    seq_index = lax.axis_index("seq")
    kv_index = lax.axis_index("kv")
    stretch = activations.shape[1]
    width_part = MODEL_WIDTH // lax.axis_size("kv")
    heads_local = query_projection_weight.shape[1] // HEAD_SIZE
    kv_local = key_value_weight.shape[2] // HEAD_SIZE
    begin = seq_index * stretch
    maps_query = hedgehog_maps[0]
    maps_key = hedgehog_maps[1]
    outputs = []
    grad_inputs = []
    big_total = None
    small_total = None
    for batch_index in range(MB):
        full_weights = (
            lax.all_gather(norm_gain_pair, "seq", axis=1, tiled=True),
            lax.all_gather(query_projection_weight, "seq", axis=0, tiled=True),
            lax.all_gather(key_value_weight, "seq", axis=1, tiled=True),
            lax.all_gather(output_projection_weight, "seq", axis=1, tiled=True),
            lax.all_gather(gate_up_weight, "seq", axis=1, tiled=True),
            lax.all_gather(down_weight, "seq", axis=1, tiled=True),
            lax.all_gather(adapter_down_maps, "seq", axis=0, tiled=True),
            lax.all_gather(output_adapter_up, "seq", axis=1, tiled=True),
        )
        (
            gains_full,
            query_weight,
            keyval_weight,
            projection_weight,
            gateup_w,
            down_w,
            enter_w,
            expand_w,
        ) = full_weights
        gain_one = gains_full[0].astype(jnp.float32)
        gain_two = gains_full[1].astype(jnp.float32)
        inputs_f = activations[batch_index].astype(jnp.float32)
        cot_rows = cotangent[batch_index]
        scale_one = rms_scale(inputs_f)
        first_normed = (inputs_f * scale_one * gain_one).astype(jnp.bfloat16)
        adapter_apply = product_value(first_normed, enter_w).astype(jnp.bfloat16)
        query_second = (
            product_value(first_normed, query_weight)
            + product_value(adapter_apply[:, :ADAPTER_RANK], query_adapter_up)
        ).astype(jnp.bfloat16)
        key_b = (
            product_value(first_normed, keyval_weight[0])
            + product_value(adapter_apply[:, ADAPTER_RANK : 2 * ADAPTER_RANK], keyval_adapter_up[0])
        ).astype(jnp.bfloat16)
        value_b = (
            product_value(first_normed, keyval_weight[1])
            + product_value(adapter_apply[:, 2 * ADAPTER_RANK :], keyval_adapter_up[1])
        ).astype(jnp.bfloat16)
        halo_key, halo_value = passed_along(
            (key_b[stretch - WIN :], value_b[stretch - WIN :]), "seq", 1
        )
        key_ext = (
            jnp.concatenate([halo_key, key_b], axis=0)
            .astype(jnp.float32)
            .reshape(stretch + WIN, kv_local, HEAD_SIZE)
        )
        value_ext = (
            jnp.concatenate([halo_value, value_b], axis=0)
            .astype(jnp.float32)
            .reshape(stretch + WIN, kv_local, HEAD_SIZE)
        )
        query_in = query_second.astype(jnp.float32).reshape(stretch, heads_local, HEAD_SIZE)
        starts = document_starts[batch_index]
        pos_query = begin + jnp.arange(stretch, dtype=jnp.int32)
        pos_key = begin - WIN + jnp.arange(stretch + WIN, dtype=jnp.int32)
        doc_query = doc_of(starts, pos_query)
        doc_key = doc_of(starts, pos_key)
        doc_before = doc_of(starts, jnp.reshape(begin - WIN - 1, (1,)))[0]
        gap_size = pos_query[:, None] - pos_key[None, :]
        same_doc = doc_query[:, None] == doc_key[None, :]
        near_mask = same_doc & (gap_size >= 0) & (gap_size < WIN)
        distant_mask = same_doc & (gap_size >= WIN)
        use_state = (doc_query == doc_before).astype(jnp.float32)
        last_doc = doc_key[stretch - 1]
        keep_mask = (doc_key[:stretch] == last_doc).astype(jnp.float32)
        pass_flag = (last_doc == doc_before).astype(jnp.float32)
        (key_rep, feature_key), pull_key = jax.vjp(key_side, key_ext, maps_key)

        def range_terms(feat_range, value_range):
            return state_terms(feat_range, value_range, keep_mask)

        (state_own, norm_own), pull_state = jax.vjp(
            range_terms, feature_key[:stretch], value_ext[:stretch]
        )
        identity = (jnp.zeros_like(state_own), jnp.zeros_like(norm_own), jnp.ones((), jnp.float32))
        previous_state, norm_prev, unused_flag = prefix(
            (state_own, norm_own, pass_flag), "seq", mix_states, identity
        )

        def attend_here(query_arg, key_arg, value_arg, maps_arg, feat_arg, state_arg, norm_arg):
            return attend(
                query_arg,
                key_arg,
                value_arg,
                maps_arg,
                feat_arg,
                state_arg,
                norm_arg,
                near_mask,
                distant_mask,
                use_state,
            )

        attended, pull_attend = jax.vjp(
            attend_here,
            query_in,
            key_rep,
            value_ext,
            maps_query,
            feature_key,
            previous_state,
            norm_prev,
        )
        attention_second = attended.reshape(stretch, heads_local * HEAD_SIZE).astype(jnp.bfloat16)
        project_sum, reduce_sum = lax.psum(
            (
                product_value(attention_second, projection_weight),
                product_value(attention_second, output_adapter_down),
            ),
            "kv",
        )
        reduce_b = reduce_sum.astype(jnp.bfloat16)
        resid = inputs_f + project_sum + product_value(reduce_b, expand_w)
        scale_two = rms_scale(resid)
        normed_two = (resid * scale_two * gain_two).astype(jnp.bfloat16)
        gate = product_value(normed_two, gateup_w[0])
        upper = product_value(normed_two, gateup_w[1])
        sigma = jax.nn.sigmoid(gate)
        silu_gate = gate * sigma
        hidden_b = (silu_gate * upper).astype(jnp.bfloat16)
        down_share = lax.psum_scatter(
            product_value(hidden_b, down_w).astype(jnp.bfloat16),
            "kv",
            scatter_dimension=1,
            tiled=True,
        ).astype(jnp.float32)
        resid_share = lax.dynamic_slice_in_dim(resid, kv_index * width_part, width_part, 1)
        outputs.append((resid_share + down_share).astype(jnp.bfloat16))
        d_hidden = jnp.einsum("td,fd->tf", cot_rows, down_w, preferred_element_type=jnp.float32)
        grad_down_local = jnp.einsum(
            "tf,td->fd", hidden_b, cot_rows, preferred_element_type=jnp.float32
        )
        d_gate = (d_hidden * upper * (sigma * (1.0 + gate * (1.0 - sigma)))).astype(jnp.bfloat16)
        d_upper = (d_hidden * silu_gate).astype(jnp.bfloat16)
        grad_gateup_local = jnp.stack(
            [
                jnp.einsum("td,tf->df", normed_two, d_gate, preferred_element_type=jnp.float32),
                jnp.einsum("td,tf->df", normed_two, d_upper, preferred_element_type=jnp.float32),
            ]
        )
        norm_two_part = jnp.einsum(
            "tf,df->td", d_gate, gateup_w[0], preferred_element_type=jnp.float32
        ) + jnp.einsum("tf,df->td", d_upper, gateup_w[1], preferred_element_type=jnp.float32)
        d_normed_two = lax.psum(norm_two_part, "kv")
        grad_gain_two = jnp.sum(d_normed_two * resid * scale_two, axis=0)
        weighted_two = gain_two * d_normed_two
        d_resid = (
            cot_rows.astype(jnp.float32)
            + scale_two * weighted_two
            - resid * scale_two**3 * jnp.mean(weighted_two * resid, axis=-1, keepdims=True)
        )
        d_branch = d_resid.astype(jnp.bfloat16)
        grad_project_local = jnp.einsum(
            "ta,td->ad", attention_second, d_branch, preferred_element_type=jnp.float32
        )
        grad_expand_local = jnp.einsum(
            "tr,td->rd", reduce_b, d_branch, preferred_element_type=jnp.float32
        )
        reduce_gradient = jnp.einsum(
            "td,rd->tr", d_branch, expand_w, preferred_element_type=jnp.float32
        )
        attn_f = attention_second.astype(jnp.float32)
        reduce_gradient_part = jnp.einsum(
            "ta,tr->ar", attn_f, reduce_gradient, precision=EXACT_MODE
        )
        d_attn = (
            jnp.einsum("td,ad->ta", d_branch, projection_weight, preferred_element_type=jnp.float32)
            + jnp.einsum(
                "sy,by->sb",
                reduce_gradient,
                output_adapter_down.astype(jnp.float32),
                precision=EXACT_MODE,
            )
        ).astype(jnp.bfloat16)
        d_attended = d_attn.astype(jnp.float32).reshape(stretch, heads_local, HEAD_SIZE)
        d_query_in, d_key_rep, d_value_one, d_maps_query, d_feat_one, d_state, d_norm = pull_attend(
            d_attended
        )
        grad_state, grad_norm, unused_pass = prefix_2(
            (d_state, d_norm, pass_flag), "seq", mix_states, identity
        )
        d_feat_range, d_value_range = pull_state((grad_state, grad_norm))
        d_feat_key = d_feat_one + jnp.concatenate(
            [d_feat_range, jnp.zeros((WIN,) + d_feat_range.shape[1:], jnp.float32)], axis=0
        )
        d_value_ext = d_value_one + jnp.concatenate(
            [d_value_range, jnp.zeros((WIN,) + d_value_range.shape[1:], jnp.float32)], axis=0
        )
        d_key_ext, d_maps_key = pull_key((d_key_rep, d_feat_key))
        back_key, back_value = (
            passed_along(d_key_ext[:WIN].astype(jnp.bfloat16), "seq", -1).astype(jnp.float32),
            passed_along(d_value_ext[:WIN].astype(jnp.bfloat16), "seq", -1).astype(jnp.float32),
        )
        key_gradient = (
            jnp.concatenate([d_key_ext[WIN:stretch], d_key_ext[stretch:] + back_key], axis=0)
            .reshape(stretch, kv_local * HEAD_SIZE)
            .astype(jnp.bfloat16)
        )
        value_gradient = (
            jnp.concatenate([d_value_ext[WIN:stretch], d_value_ext[stretch:] + back_value], axis=0)
            .reshape(stretch, kv_local * HEAD_SIZE)
            .astype(jnp.bfloat16)
        )
        query_gradient = d_query_in.reshape(stretch, heads_local * HEAD_SIZE).astype(jnp.bfloat16)
        grad_query_local = jnp.einsum(
            "td,ta->da", first_normed, query_gradient, preferred_element_type=jnp.float32
        )
        grad_keyval_local = jnp.stack(
            [
                jnp.einsum(
                    "td,ta->da", first_normed, key_gradient, preferred_element_type=jnp.float32
                ),
                jnp.einsum(
                    "td,ta->da", first_normed, value_gradient, preferred_element_type=jnp.float32
                ),
            ]
        )
        query_adapter_gradient_part = jnp.einsum(
            "tr,ta->ra",
            adapter_apply[:, :ADAPTER_RANK],
            query_gradient,
            preferred_element_type=jnp.float32,
        )
        keyval_adapter_gradient_part = jnp.stack(
            [
                jnp.einsum(
                    "tr,ta->ra",
                    adapter_apply[:, ADAPTER_RANK : 2 * ADAPTER_RANK],
                    key_gradient,
                    preferred_element_type=jnp.float32,
                ),
                jnp.einsum(
                    "tr,ta->ra",
                    adapter_apply[:, 2 * ADAPTER_RANK :],
                    value_gradient,
                    preferred_element_type=jnp.float32,
                ),
            ]
        )
        adapt_part = jnp.concatenate(
            [
                jnp.einsum(
                    "og,zg->oz",
                    query_gradient,
                    query_adapter_up,
                    preferred_element_type=jnp.float32,
                ),
                jnp.einsum(
                    "og,zg->oz",
                    key_gradient,
                    keyval_adapter_up[0],
                    preferred_element_type=jnp.float32,
                ),
                jnp.einsum(
                    "og,zg->oz",
                    value_gradient,
                    keyval_adapter_up[1],
                    preferred_element_type=jnp.float32,
                ),
            ],
            axis=1,
        )
        norm_one_part = (
            jnp.einsum(
                "ta,da->td", query_gradient, query_weight, preferred_element_type=jnp.float32
            )
            + jnp.einsum(
                "ta,da->td", key_gradient, keyval_weight[0], preferred_element_type=jnp.float32
            )
            + jnp.einsum(
                "ta,da->td", value_gradient, keyval_weight[1], preferred_element_type=jnp.float32
            )
        )
        d_normed_part, d_adapt = (
            lax.psum(norm_one_part.astype(jnp.bfloat16), "kv").astype(jnp.float32),
            lax.psum(adapt_part.astype(jnp.bfloat16), "kv").astype(jnp.float32),
        )
        d_normed_one = d_normed_part + jnp.einsum(
            "tr,dr->td", d_adapt, enter_w.astype(jnp.float32), precision=EXACT_MODE
        )
        grad_enter_local = jnp.einsum(
            "td,tr->dr", first_normed.astype(jnp.float32), d_adapt, precision=EXACT_MODE
        )
        grad_gain_one = jnp.sum(d_normed_one * inputs_f * scale_one, axis=0)
        weighted_one = gain_one * d_normed_one
        d_inputs = (
            d_resid
            + scale_one * weighted_one
            - inputs_f * scale_one**3 * jnp.mean(weighted_one * inputs_f, axis=-1, keepdims=True)
        )
        grad_inputs.append(d_inputs)
        grad_gains_local = jnp.stack([grad_gain_one, grad_gain_two])
        maps_gradient_part = jnp.stack([d_maps_query, d_maps_key])
        big_part = (
            lax.psum_scatter(
                grad_gains_local.astype(jnp.bfloat16), "seq", scatter_dimension=1, tiled=True
            ).astype(jnp.float32),
            lax.psum_scatter(
                grad_query_local.astype(jnp.bfloat16), "seq", scatter_dimension=0, tiled=True
            ).astype(jnp.float32),
            lax.psum_scatter(
                grad_keyval_local.astype(jnp.bfloat16), "seq", scatter_dimension=1, tiled=True
            ).astype(jnp.float32),
            lax.psum_scatter(
                grad_project_local.astype(jnp.bfloat16), "seq", scatter_dimension=1, tiled=True
            ).astype(jnp.float32),
            lax.psum_scatter(
                grad_gateup_local.astype(jnp.bfloat16), "seq", scatter_dimension=1, tiled=True
            ).astype(jnp.float32),
            lax.psum_scatter(
                grad_down_local.astype(jnp.bfloat16), "seq", scatter_dimension=1, tiled=True
            ).astype(jnp.float32),
            lax.psum_scatter(
                grad_enter_local.astype(jnp.bfloat16), "seq", scatter_dimension=0, tiled=True
            ).astype(jnp.float32),
            lax.psum_scatter(
                grad_expand_local.astype(jnp.bfloat16), "seq", scatter_dimension=1, tiled=True
            ).astype(jnp.float32),
        )
        small_part = (
            lax.psum(query_adapter_gradient_part.astype(jnp.bfloat16), "seq").astype(jnp.float32),
            lax.psum(keyval_adapter_gradient_part.astype(jnp.bfloat16), "seq").astype(jnp.float32),
            lax.psum(reduce_gradient_part.astype(jnp.bfloat16), "seq").astype(jnp.float32),
            lax.psum(maps_gradient_part.astype(jnp.bfloat16), "seq").astype(jnp.float32),
        )
        big_total = add_trees(big_total, big_part)
        small_total = add_trees(small_total, small_part)
    return (
        jnp.stack(outputs),
        jnp.stack(grad_inputs),
        big_total[0],
        big_total[1],
        big_total[2],
        big_total[3],
        big_total[4],
        big_total[5],
        big_total[6],
        small_total[0],
        small_total[1],
        small_total[2],
        big_total[7],
        small_total[3],
    )


def solution(mesh):
    placed = (
        P(None, "seq", None),
        P(None, "seq", None),
        P(),
        P(None, "seq"),
        P("seq", "kv"),
        P(None, "seq", "kv"),
        P("kv", "seq"),
        P(None, "seq", "kv"),
        P("kv", "seq"),
        P("seq", None),
        P(None, "kv"),
        P(None, None, "kv"),
        P("kv", None),
        P(None, "seq"),
        P(None, "kv", None, None),
    )
    return jax.shard_map(
        per_device,
        mesh=mesh,
        in_specs=placed,
        out_specs=(
            P(None, "seq", "kv"),
            P(None, "seq", None),
            P(None, "seq"),
            P("seq", "kv"),
            P(None, "seq", "kv"),
            P("kv", "seq"),
            P(None, "seq", "kv"),
            P("kv", "seq"),
            P("seq", None),
            P(None, "kv"),
            P(None, None, "kv"),
            P("kv", None),
            P(None, "seq"),
            P(None, "kv", None, None),
        ),
        check_vma=False,
    )
```

profile of v0, /device:TPU:0, one launch (start us, length us, event | category | flops | bytes accessed | tf_op | source)
XLA Modules:
  0.0 2105.6 jit_solution(15074421966711244110)
XLA Ops:
  75.3 12.7 all-reduce.10
  89.8 11.4 all-gather.3
  145.1 12.3 select_reduce_fusion.1
  162.9 50.2 %while.69 = (s32[]{:T(128)}, f32[8,128,64]{2,1,0:T(8,128)}, f32[8,128]{1,0:T(8,128)S(1)}, s32[]{:T(128)}, bf16[8]{0:T(256)(128)(2,1)}, /*index=5*/bf16[8,8,128,6...) while((s32[]{:T(128)}, f32[8,128,64]{2,1,0:T(8,128)}, ...), condition=%wide.region_35.36_spmd.clone, body=%wide.region_34.35_spmd.clone.sunk | while | flops 332805 | bytes 1190041 | solution.py:45
  213.1 50.8 %while.68 = (s32[]{:T(128)}, f32[8,128,64]{2,1,0:T(8,128)}, f32[8,128]{1,0:T(8,128)S(1)}, s32[]{:T(128)}, bf16[8]{0:T(256)(128)(2,1)}, /*index=5*/bf16[8,8,128,6...) while((s32[]{:T(128)}, f32[8,128,64]{2,1,0:T(8,128)}, ...), condition=%wide.region_14.15_spmd.clone, body=%wide.region_13.14_spmd.clone.sunk | while | flops 332805 | bytes 1190041 | solution.py:45
  292.4 20.1 all-reduce.6
  312.6 123.5 %all-reduce.21.cloned.1.call-done = (f32[256,2048]{1,0:T(8,128)}, f32[256,2048]{1,0:T(8,128)}) async-done(((f32[256,2048]{1,0:T(8,128)}, f32[256,2048]{1,0:T(8,128)}), (f32[256,2048]{1,0:T(8,128)}, f32[256,2048]{1,0:T(8,128)})) %all-reduce.21.cloned.1.call-update) | async-done | bytes 4194320 | tf_op jit(solution)/shard_map/psum | solution.py:301
  443.2 83.9 %all-gather.24.cloned.1.call-done = bf16[2,2048,2048]{2,1,0:T(8,128)(2,1)} async-done(((bf16[2,256,2048]{2,1,0:T(8,128)(2,1)}), bf16[2,2048,2048]{2,1,0:T(8,128)(2,1)}) %all-gather.24.cloned.1.call-update) | async-done | bytes 16777232 | tf_op jit(solution)/shard_map/all_gather | solution.py:201
  550.8 34.3 %all-gather.26.cloned.1.call-done = bf16[2048,2048]{1,0:T(8,128)(2,1)} async-done(((bf16[2048,256]{1,0:T(8,128)(2,1)}), bf16[2048,2048]{1,0:T(8,128)(2,1)}) %all-gather.26.cloned.1.call-update) | async-done | bytes 8388624 | tf_op jit(solution)/shard_map/all_gather | solution.py:202
  633.8 150.0 %all-reduce.19.cloned.1.call-done = (f32[256,2048]{1,0:T(8,128)}, f32[256,2048]{1,0:T(8,128)}) async-done(((f32[256,2048]{1,0:T(8,128)}, f32[256,2048]{1,0:T(8,128)}), (f32[256,2048]{1,0:T(8,128)}, f32[256,2048]{1,0:T(8,128)})) %all-reduce.19.cloned.1.call-update) | async-done | bytes 4194320 | tf_op jit(solution)/shard_map/psum | solution.py:340
  876.3 55.1 %while.71 = (s32[]{:T(128)}, f32[8,128,64]{2,1,0:T(8,128)}, f32[8,128]{1,0:T(8,128)}, s32[]{:T(128)}, bf16[8]{0:T(256)(128)(2,1)}, /*index=5*/bf16[8,8,128,64]{2...) while((s32[]{:T(128)}, f32[8,128,64]{2,1,0:T(8,128)}, ...), condition=%wide.region_63.64_spmd.clone, body=%wide.region_62.63_spmd.clone.sunk | while | flops 332809 | bytes 1190103 | solution.py:69
  947.5 56.0 %while.70 = (s32[]{:T(128)}, f32[8,128,64]{2,1,0:T(8,128)}, f32[8,128]{1,0:T(8,128)}, s32[]{:T(128)}, bf16[8]{0:T(256)(128)(2,1)}, /*index=5*/bf16[8,8,128,64]{2...) while((s32[]{:T(128)}, f32[8,128,64]{2,1,0:T(8,128)}, ...), condition=%wide.region_48.49_spmd.clone, body=%wide.region_47.48_spmd.clone.sunk | while | flops 332809 | bytes 1190103 | solution.py:69
  1059.8 18.3 all-reduce.12
  1102.3 17.2 all-reduce.25.cloned.1.call-done
  1180.5 28.7 %reduce-scatter.53.cloned.1.call-done = bf16[8,256]{1,0:T(8,128)(2,1)} async-done(((bf16[8,2048]{1,0:T(8,128)(2,1)}), bf16[8,256]{1,0:T(8,128)(2,1)}) %reduce-scatter.53.cloned.1.call-update) | async-done | bytes 4112 | tf_op jit(solution)/shard_map/reduce_scatter | solution.py:512
  1209.1 34.2 %reduce-scatter.51.cloned.1.call-done = bf16[8,256]{1,0:T(8,128)(2,1)} async-done(((bf16[8,2048]{1,0:T(8,128)(2,1)}), bf16[8,256]{1,0:T(8,128)(2,1)}) %reduce-scatter.51.cloned.1.call-update) | async-done | bytes 4112 | tf_op jit(solution)/shard_map/reduce_scatter | solution.py:512
  1251.6 23.1 %all-reduce.9 = (bf16[8,512]{1,0:T(8,128)(2,1)S(1)}, bf16[8,512]{1,0:T(8,128)(2,1)S(1)}, bf16[2,8,128]{2,1,0:T(8,128)(2,1)S(1)}, bf16[2,8,128]{2,1,0:T(8,128)(2,...) all-reduce(bf16[8,512]{1,0:T(8,128)(2,1)S(1)} %convolution_convert_, ...), channel_id=1, replica_groups=mesh['seq'=8,'kv'=4] {'seq'}, use_global_device_ids=true, to_apply=%region_91.92 | all-reduce | flops 20480 | bytes 81920 | tf_op jit(solution)/shard_map/psum | solution.py:517
  1276.5 26.1 %all-reduce.23.cloned.1.call-done = (bf16[2,8,64,64]{3,2,1,0:T(8,128)(2,1)}, bf16[2,8,64,64]{3,2,1,0:T(8,128)(2,1)}) async-done(((bf16[2,8,64,64]{3,2,1,0:T(8,128)(2,1)}, bf16[2,8,64,64]{3,2,1,0:T(8,128)(2,1)}), (bf16[2,8,64,64]{3,2,1,0:T(8,128)(2,1)}, bf16[2,8,64,64]{3,2,1,0:T(8,128)(2,1)})) %all-reduce.23.cloned.1.call-update) | async-done | bytes 262160 | tf_op jit(solution)/shard_map/psum | solution.py:520
  1304.4 33.3 %reduce-scatter.49.cloned.1.call-done = bf16[256,24]{0,1:T(8,128)(2,1)} async-done(((bf16[2048,24]{0,1:T(8,128)(2,1)}), bf16[256,24]{0,1:T(8,128)(2,1)}) %reduce-scatter.49.cloned.1.call-update) | async-done | bytes 12304 | tf_op jit(solution)/shard_map/reduce_scatter | solution.py:509
  1337.7 35.4 %reduce-scatter.47.cloned.1.call-done = bf16[256,24]{0,1:T(8,128)(2,1)} async-done(((bf16[2048,24]{0,1:T(8,128)(2,1)}), bf16[256,24]{0,1:T(8,128)(2,1)}) %reduce-scatter.47.cloned.1.call-update) | async-done | bytes 12304 | tf_op jit(solution)/shard_map/reduce_scatter | solution.py:509
  1374.5 43.1 %reduce-scatter.29.cloned.1.call-done = bf16[256,512]{1,0:T(8,128)(2,1)} async-done(((bf16[2048,512]{1,0:T(8,128)(2,1)}), bf16[256,512]{1,0:T(8,128)(2,1)}) %reduce-scatter.29.cloned.1.call-update) | async-done | bytes 262160 | tf_op jit(solution)/shard_map/reduce_scatter | solution.py:494
  1417.6 44.9 %reduce-scatter.27.cloned.1.call-done = bf16[256,512]{1,0:T(8,128)(2,1)} async-done(((bf16[2048,512]{1,0:T(8,128)(2,1)}), bf16[256,512]{1,0:T(8,128)(2,1)}) %reduce-scatter.27.cloned.1.call-update) | async-done | bytes 262160 | tf_op jit(solution)/shard_map/reduce_scatter | solution.py:494
  1464.4 42.6 %reduce-scatter.37.cloned.1.call-done = bf16[512,256]{1,0:T(8,128)(2,1)} async-done(((bf16[512,2048]{1,0:T(8,128)(2,1)}), bf16[512,256]{1,0:T(8,128)(2,1)}) %reduce-scatter.37.cloned.1.call-update) | async-done | bytes 262160 | tf_op jit(solution)/shard_map/reduce_scatter | solution.py:500
  1507.0 44.9 %reduce-scatter.35.cloned.1.call-done = bf16[512,256]{1,0:T(8,128)(2,1)} async-done(((bf16[512,2048]{1,0:T(8,128)(2,1)}), bf16[512,256]{1,0:T(8,128)(2,1)}) %reduce-scatter.35.cloned.1.call-update) | async-done | bytes 262160 | tf_op jit(solution)/shard_map/reduce_scatter | solution.py:500
  1553.8 37.2 %reduce-scatter.33.cloned.1.call-done = bf16[2,256,128]{2,1,0:T(8,128)(2,1)} async-done(((bf16[2,2048,128]{2,1,0:T(8,128)(2,1)}), bf16[2,256,128]{2,1,0:T(8,128)(2,1)}) %reduce-scatter.33.cloned.1.call-update) | async-done | bytes 131088 | tf_op jit(solution)/shard_map/reduce_scatter | solution.py:497
  1591.0 39.2 %reduce-scatter.31.cloned.1.call-done = bf16[2,256,128]{2,1,0:T(8,128)(2,1)} async-done(((bf16[2,2048,128]{2,1,0:T(8,128)(2,1)}), bf16[2,256,128]{2,1,0:T(8,128)(2,1)}) %reduce-scatter.31.cloned.1.call-update) | async-done | bytes 131088 | tf_op jit(solution)/shard_map/reduce_scatter | solution.py:497
  1638.3 28.9 %reduce-scatter.57.cloned.1.call-done = bf16[256,2]{1,0:T(8,128)(2,1)} async-done(((bf16[2048,2]{1,0:T(8,128)(2,1)}), bf16[256,2]{1,0:T(8,128)(2,1)}) %reduce-scatter.57.cloned.1.call-update) | async-done | bytes 1040
  1668.1 36.5 %reduce-scatter.55.cloned.1.call-done = bf16[256,2]{1,0:T(8,128)(2,1)} async-done(((bf16[2048,2]{1,0:T(8,128)(2,1)}), bf16[256,2]{1,0:T(8,128)(2,1)}) %reduce-scatter.55.cloned.1.call-update) | async-done | bytes 1040
  1706.1 73.2 %reduce-scatter.45.cloned.1.call-done = bf16[2048,256]{1,0:T(8,128)(2,1)} async-done(((bf16[2048,2048]{1,0:T(8,128)(2,1)}), bf16[2048,256]{1,0:T(8,128)(2,1)}) %reduce-scatter.45.cloned.1.call-update) | async-done | bytes 1048592 | tf_op jit(solution)/shard_map/reduce_scatter | solution.py:506
  1779.4 75.2 %reduce-scatter.43.cloned.1.call-done = bf16[2048,256]{1,0:T(8,128)(2,1)} async-done(((bf16[2048,2048]{1,0:T(8,128)(2,1)}), bf16[2048,256]{1,0:T(8,128)(2,1)}) %reduce-scatter.43.cloned.1.call-update) | async-done | bytes 1048592 | tf_op jit(solution)/shard_map/reduce_scatter | solution.py:506
  1857.6 116.3 %reduce-scatter.41.cloned.1.call-done = bf16[2,256,2048]{2,1,0:T(8,128)(2,1)} async-done(((bf16[2,2048,2048]{2,1,0:T(8,128)(2,1)}), bf16[2,256,2048]{2,1,0:T(8,128)(2,1)}) %reduce-scatter.41.cloned.1.call-update) | async-done | bytes 2097168 | tf_op jit(solution)/shard_map/reduce_scatter | solution.py:503
  1973.9 119.5 %reduce-scatter.39.cloned.1.call-done = bf16[2,256,2048]{2,1,0:T(8,128)(2,1)} async-done(((bf16[2,2048,2048]{2,1,0:T(8,128)(2,1)}), bf16[2,256,2048]{2,1,0:T(8,128)(2,1)}) %reduce-scatter.39.cloned.1.call-update) | async-done | bytes 2097168 | tf_op jit(solution)/shard_map/reduce_scatter | solution.py:503
  (1189 shorter events, 696.3 us)
Async XLA Ops:
  7.2 29.5 %all-gather.18.cloned.1.call-start = ((), (), s32[]{:S(2)}) async-start(), calls=%async_computation.18 | async-start | bytes 1179648 | tf_op jit(solution)/shard_map/all_gather | solution.py:199
  8.0 104.2 %all-gather.20.cloned.1.call-start = ((), (), s32[]{:S(2)}) async-start(), calls=%async_computation.19 | async-start | bytes 2359296 | tf_op jit(solution)/shard_map/all_gather | solution.py:198
  8.7 154.2 %all-gather.30.cloned.1.call-start = ((), (), s32[]{:S(2)}) async-start(), calls=%async_computation.40 | async-start | bytes 1179648 | tf_op jit(solution)/shard_map/all_gather | solution.py:28
  55.0 158.1 %all-gather.28.cloned.1.call-start = ((), (), s32[]{:S(2)}) async-start(), calls=%async_computation.39 | async-start | bytes 1179648 | tf_op jit(solution)/shard_map/all_gather | solution.py:28
  67.0 206.5 %all-gather.22.cloned.1.call-start = ((), (), s32[]{:S(2)}) async-start(), calls=%async_computation.20 | async-start | bytes 2359296 | tf_op jit(solution)/shard_map/all_gather | solution.py:200
  67.6 368.5 %all-reduce.21.cloned.1.call-start = ((), (), s32[]{:S(2)}) async-start(), calls=%async_computation.46 | async-start | bytes 8388608 | tf_op jit(solution)/shard_map/psum | solution.py:301
  279.6 247.5 %all-gather.24.cloned.1.call-start = ((), (), s32[]{:S(2)}) async-start(), calls=%async_computation.21 | async-start | bytes 18874368 | tf_op jit(solution)/shard_map/all_gather | solution.py:201
  280.3 304.8 %all-gather.26.cloned.1.call-start = ((), (), s32[]{:S(2)}) async-start(), calls=%async_computation.22 | async-start | bytes 9437184 | tf_op jit(solution)/shard_map/all_gather | solution.py:202
  281.1 502.7 %all-reduce.19.cloned.1.call-start = ((), (), s32[]{:S(2)}) async-start(), calls=%async_computation.45 | async-start | bytes 8388608 | tf_op jit(solution)/shard_map/psum | solution.py:340
  628.3 248.0 %all-gather.34.cloned.1.call-start = ((), (), s32[]{:S(2)}) async-start(), calls=%async_computation.42 | async-start | bytes 1179648 | tf_op jit(solution)/shard_map/all_gather | solution.py:51
  823.1 124.4 %all-gather.32.cloned.1.call-start = ((), (), s32[]{:S(2)}) async-start(), calls=%async_computation.41 | async-start | bytes 1179648 | tf_op jit(solution)/shard_map/all_gather | solution.py:51
  876.2 243.3 %all-reduce.25.cloned.1.call-start = ((), (), s32[]{:S(2)}) async-start(), calls=%async_computation.48 | async-start | bytes 4194304 | tf_op jit(solution)/shard_map/psum | solution.py:471
  935.7 84.3 %collective-permute-start.7 = (bf16[64,2,64]{0,2,1:T(8,128)(2,1)}, bf16[64,2,64]{0,2,1:T(8,128)(2,1)}, u32[]{:S(2)}, u32[]{:S(2)}) collective-permute-start(bf16[64,2,64]{0,2,1:T(8,128)(2,1)} %slice.454), channel_id=1, source_target_pairs={{4,0},{8,4},{12,8},{16,12},{20,16},{24,20},{28,24},{5,1},{9,5},{13... | collective-permute-start | bytes 49160 | tf_op jit(solution)/shard_map/ppermute | solution.py:22
  1029.7 142.4 %reduce-scatter.25.cloned.1.call-start = ((), (), s32[]{:S(2)}) async-start(), calls=%async_computation.24 | async-start | bytes 1310720 | tf_op jit(solution)/shard_map/reduce_scatter | solution.py:317
  1037.8 138.3 %reduce-scatter.23.cloned.1.call-start = ((), (), s32[]{:S(2)}) async-start(), calls=%async_computation.23 | async-start | bytes 1310720 | tf_op jit(solution)/shard_map/reduce_scatter | solution.py:317
  1044.8 164.4 %reduce-scatter.53.cloned.1.call-start = ((), (), s32[]{:S(2)}) async-start(), calls=%async_computation.38 | async-start | bytes 36864 | tf_op jit(solution)/shard_map/reduce_scatter | solution.py:512
  1052.2 191.1 %reduce-scatter.51.cloned.1.call-start = ((), (), s32[]{:S(2)}) async-start(), calls=%async_computation.37 | async-start | bytes 36864 | tf_op jit(solution)/shard_map/reduce_scatter | solution.py:512
  1053.8 248.8 %all-reduce.23.cloned.1.call-start = ((), (), s32[]{:S(2)}) async-start(), calls=%async_computation.47 | async-start | bytes 1048576 | tf_op jit(solution)/shard_map/psum | solution.py:520
  1058.9 278.8 %reduce-scatter.49.cloned.1.call-start = ((), (), s32[]{:S(2)}) async-start(), calls=%async_computation.36 | async-start | bytes 110592 | tf_op jit(solution)/shard_map/reduce_scatter | solution.py:509
  1080.5 292.6 %reduce-scatter.47.cloned.1.call-start = ((), (), s32[]{:S(2)}) async-start(), calls=%async_computation.35 | async-start | bytes 110592 | tf_op jit(solution)/shard_map/reduce_scatter | solution.py:509
  1083.0 334.6 %reduce-scatter.29.cloned.1.call-start = ((), (), s32[]{:S(2)}) async-start(), calls=%async_computation.26 | async-start | bytes 2359296 | tf_op jit(solution)/shard_map/reduce_scatter | solution.py:494
  1086.9 375.6 %reduce-scatter.27.cloned.1.call-start = ((), (), s32[]{:S(2)}) async-start(), calls=%async_computation.25 | async-start | bytes 2359296 | tf_op jit(solution)/shard_map/reduce_scatter | solution.py:494
  1090.4 416.6 %reduce-scatter.37.cloned.1.call-start = ((), (), s32[]{:S(2)}) async-start(), calls=%async_computation.30 | async-start | bytes 2359296 | tf_op jit(solution)/shard_map/reduce_scatter | solution.py:500
  1092.6 459.3 %reduce-scatter.35.cloned.1.call-start = ((), (), s32[]{:S(2)}) async-start(), calls=%async_computation.29 | async-start | bytes 2359296 | tf_op jit(solution)/shard_map/reduce_scatter | solution.py:500
  1095.9 495.1 %reduce-scatter.33.cloned.1.call-start = ((), (), s32[]{:S(2)}) async-start(), calls=%async_computation.28 | async-start | bytes 1179648 | tf_op jit(solution)/shard_map/reduce_scatter | solution.py:497
  1099.1 531.1 %reduce-scatter.31.cloned.1.call-start = ((), (), s32[]{:S(2)}) async-start(), calls=%async_computation.27 | async-start | bytes 1179648 | tf_op jit(solution)/shard_map/reduce_scatter | solution.py:497
  1101.6 565.6 %reduce-scatter.57.cloned.1.call-start = ((), (), s32[]{:S(2)}) async-start(), calls=%async_computation.44 | async-start | bytes 589824
  1127.1 577.6 %reduce-scatter.55.cloned.1.call-start = ((), (), s32[]{:S(2)}) async-start(), calls=%async_computation.43 | async-start | bytes 589824
  1128.9 650.4 %reduce-scatter.45.cloned.1.call-start = ((), (), s32[]{:S(2)}) async-start(), calls=%async_computation.34 | async-start | bytes 9437184 | tf_op jit(solution)/shard_map/reduce_scatter | solution.py:506
  1135.9 718.7 %reduce-scatter.43.cloned.1.call-start = ((), (), s32[]{:S(2)}) async-start(), calls=%async_computation.33 | async-start | bytes 9437184 | tf_op jit(solution)/shard_map/reduce_scatter | solution.py:506
  1143.9 830.0 %reduce-scatter.41.cloned.1.call-start = ((), (), s32[]{:S(2)}) async-start(), calls=%async_computation.32 | async-start | bytes 18874368 | tf_op jit(solution)/shard_map/reduce_scatter | solution.py:503
  1157.9 935.5 %reduce-scatter.39.cloned.1.call-start = ((), (), s32[]{:S(2)}) async-start(), calls=%async_computation.31 | async-start | bytes 18874368 | tf_op jit(solution)/shard_map/reduce_scatter | solution.py:503
  (323 other events, 6126.6 us)
Sparse Core Ops, SparseCore 0:
  10.0 26.4 all-gather.17
  38.3 28.0 all-gather.19
  68.3 23.5 all-gather.29
  93.7 23.4 all-gather.27
  118.9 28.2 all-gather.21
  279.7 156.4 all-reduce.20
  438.2 88.8 all-gather.23
  529.1 55.9 all-gather.25
  628.4 155.3 all-reduce.18
  823.2 22.4 all-gather.33
  876.4 21.5 all-gather.31
  1029.9 89.6 all-reduce.24
  1121.9 26.1 reduce-scatter.24
  1150.2 25.7 reduce-scatter.22
  1179.2 29.9 reduce-scatter.52
  1212.0 31.2 reduce-scatter.50
  1247.8 54.7 all-reduce.22
  1306.0 31.6 reduce-scatter.48
  1340.7 32.3 reduce-scatter.46
  1376.3 41.2 reduce-scatter.28
  1421.2 41.2 reduce-scatter.26
  1465.7 41.1 reduce-scatter.36
  1510.6 41.2 reduce-scatter.34
  1554.9 35.9 reduce-scatter.32
  1594.1 35.9 reduce-scatter.30
  1633.1 34.0 reduce-scatter.56
  1670.4 34.1 reduce-scatter.54
  1708.1 71.2 reduce-scatter.44
  1783.2 71.2 reduce-scatter.42
  1858.0 115.9 reduce-scatter.40
  1977.5 115.9 reduce-scatter.38
where the time goes:
time: 2120 us; the launch traced here: 2110 us
  waiting for transfers between devices  1280 us (60%)
  matrix products  296 us (14%)
  other arithmetic  193 us (9%)
  blocking collectives  143 us (7%)
  local copies, waits for them, and re-layouts  134 us (6%)
  loops' own time  21.7 us (1%)
  between operations  21.6 us (1%)
    reduce_scatter x2, waiting for transfers between devices, per_device(): lax.psum_scatter(grad_gateup_local.astype(jnp.bfloat16), 'seq', scatter_d...  236 us
    psum x1, waiting for transfers between devices, per_device(): d_normed_two = lax.psum(norm_two_part, 'kv')  150 us
    reduce_scatter x2, waiting for transfers between devices, per_device(): lax.psum_scatter(grad_down_local.astype(jnp.bfloat16), 'seq', scatter_dim...  148 us
    psum x1, waiting for transfers between devices, per_device(): lax.psum((product_value(attention_second, projection_weight), product_val...  124 us
    select_n x64, other arithmetic, turn(): return jax.tree.map(lambda a, b: jnp.where(reached, a, b), new, before)  95.1 us
    reduce_scatter x2, waiting for transfers between devices, per_device(): lax.psum_scatter(grad_query_local.astype(jnp.bfloat16), 'seq', scatter_di...  88 us
    reduce_scatter x2, waiting for transfers between devices, per_device(): lax.psum_scatter(grad_project_local.astype(jnp.bfloat16), 'seq', scatter_...  87.5 us
    all_gather x1, waiting for transfers between devices, per_device(): lax.all_gather(gate_up_weight, 'seq', axis=1, tiled=True)  83.9 us
  transfers between devices with their start and end apart: 39, of which 26 were waited for; matrix products, arithmetic and copies ran while one was open for 24% of the time, Pallas kernels for 0%

commit v1 on v0

v1 whole, which is shorter than its diff:
```python
import functools

import jax
import jax.numpy as jnp
from jax import lax
from jax.experimental import pallas as pl
from jax.experimental.pallas import tpu as pltpu
from jax.sharding import PartitionSpec as P

MODEL_WIDTH = 2048
HEAD_SIZE = 64
ADAPTER_RANK = 8
WIN = 64
MB = 2
EPSILON = 1e-05
AUG = 80
F32 = jnp.float32
BF16 = jnp.bfloat16
VMEM_LIMIT = 56 * 1024 * 1024


def contract(left, right, dims):
    return lax.dot_general(left, right, (dims, ((), ())), preferred_element_type=F32)


def nn(left, right):
    return contract(left, right, ((1,), (0,)))


def nt(left, right):
    return contract(left, right, ((1,), (1,)))


def tn(left, right):
    return contract(left, right, ((0,), (0,)))


def cost(micros):
    return pl.CostEstimate(flops=int(micros * 1.1e9), bytes_accessed=1 << 20, transcendentals=0)


def params(count):
    return pltpu.CompilerParams(
        dimension_semantics=("arbitrary",) * count, vmem_limit_bytes=VMEM_LIMIT
    )


def flip(value, axis, bit):
    count = lax.axis_size(axis)
    return lax.ppermute(value, axis, [(i, i ^ bit) for i in range(count)])


def shift(value, axis, steps):
    count = lax.axis_size(axis)
    first, last = max(0, -steps), min(count, count - steps)
    return lax.ppermute(value, axis, [(i, i + steps) for i in range(first, last)])


def sum_all(value, axis):
    count = lax.axis_size(axis)
    value = value.astype(F32)
    for k in range(count.bit_length() - 1):
        narrow = value.astype(BF16)
        value = narrow.astype(F32) + flip(narrow, axis, 1 << k).astype(F32)
    return value


def sum_once(value, axis):
    count = lax.axis_size(axis)
    narrow = value.astype(BF16)
    terms = [narrow.astype(F32)] + [flip(narrow, axis, k).astype(F32) for k in range(1, count)]
    while len(terms) > 1:
        terms = [terms[k] + terms[k + 1] for k in range(0, len(terms), 2)]
    return terms[0]


def together(*values):
    return lax.optimization_barrier(values)


def scatter_lanes(value, axis):
    count, me = lax.axis_size(axis), lax.axis_index(axis)
    bit = count // 2
    while bit:
        cut = value.shape[1] // 2
        high = (me & bit) != 0
        kept = jnp.where(high, value[:, cut:], value[:, :cut])
        sent = jnp.where(high, value[:, :cut], value[:, cut:])
        value = kept + flip(sent.astype(BF16), axis, bit).astype(F32)
        bit //= 2
    return value


def level_send(pieces, dim):
    count, level = lax.axis_size("kv"), lax.axis_index("kv")
    terms = [lax.dynamic_index_in_dim(pieces, level, dim, keepdims=False)]
    for k in range(1, count):
        sent = lax.dynamic_index_in_dim(pieces, level ^ k, dim, keepdims=False)
        terms.append(flip(sent, "kv", k))
    return terms


def total_of(terms):
    total = terms[0].astype(F32)
    for term in terms[1:]:
        total = total + term.astype(F32)
    return total


def level_spread(own):
    count = lax.axis_size("kv")
    return [own] + [flip(own, "kv", k) for k in range(1, count)]


def level_rows(pieces, dtype, gain=None):
    count, level = lax.axis_size("kv"), lax.axis_index("kv")
    m, rows, width = pieces[0].shape
    gains = [] if gain is None else [gain]

    def kernel(level_ref, *refs):
        out_ref = refs[count + len(gains)]
        for k in range(count):
            at = pl.multiple_of((level_ref[0] ^ k) * rows, rows)
            for b in range(m):
                value = refs[k][b]
                out_ref[b, pl.ds(at, rows), :] = value.astype(dtype)
                if gains:
                    wide = value.astype(F32)
                    scale = lax.rsqrt(jnp.mean(wide * wide, axis=1, keepdims=True) + EPSILON)
                    refs[-1][b, pl.ds(at, rows), :] = (wide * scale * refs[count][...]).astype(BF16)

    whole = pl.BlockSpec(memory_space=pltpu.VMEM)
    shape = (m, rows * count, width)
    found = pl.pallas_call(
        kernel,
        in_specs=[pl.BlockSpec(memory_space=pltpu.SMEM)] + [whole] * (count + len(gains)),
        out_specs=[whole] * (1 + len(gains)),
        out_shape=[jax.ShapeDtypeStruct(shape, dtype)]
        + [jax.ShapeDtypeStruct(shape, BF16)] * len(gains),
        compiler_params=pltpu.CompilerParams(vmem_limit_bytes=VMEM_LIMIT),
    )(jnp.reshape(level, (1,)), *pieces, *gains)
    found = [part.reshape(m * rows * count, width) for part in found]
    return found if gains else found[0]


def first_hops(shard):
    return [shard] + [flip(shard, "seq", k) for k in range(2, lax.axis_size("seq"), 2)]


def second_hops(own):
    other = [flip(piece, "seq", 1) for piece in own]
    return [piece for pair in zip(own, other) for piece in pair]


def ordered_rows(pieces):
    count, me = lax.axis_size("seq"), lax.axis_index("seq")
    rows, width = pieces[0].shape

    def kernel(me_ref, *refs):
        out_ref = refs[-1]
        for k in range(count):
            out_ref[pl.ds(pl.multiple_of((me_ref[0] ^ k) * rows, rows), rows), :] = refs[k][...]

    whole = pl.BlockSpec(memory_space=pltpu.VMEM)
    return pl.pallas_call(
        kernel,
        in_specs=[pl.BlockSpec(memory_space=pltpu.SMEM)] + [whole] * count,
        out_specs=whole,
        out_shape=jax.ShapeDtypeStruct((rows * count, width), pieces[0].dtype),
        compiler_params=pltpu.CompilerParams(vmem_limit_bytes=VMEM_LIMIT),
    )(jnp.reshape(me, (1,)), *pieces)


def parity_rows(left, parity):
    count = lax.axis_size("seq")
    view = left.reshape(left.shape[0], count // 2, 2, left.shape[1] // count)
    return lax.dynamic_index_in_dim(view, parity, 2, keepdims=False).reshape(left.shape[0], -1)


def chip_pair(kept, arrived):
    count, me = lax.axis_size("seq"), lax.axis_index("seq")
    pair = (kept.astype(F32) + arrived.astype(F32)).astype(BF16)
    pair = pair.reshape(count // 2, -1, pair.shape[1])
    chip = me // 2
    terms = [lax.dynamic_index_in_dim(pair, chip, 0, keepdims=False)]
    for k in range(1, count // 2):
        sent = lax.dynamic_index_in_dim(pair, chip ^ k, 0, keepdims=False)
        terms.append(flip(sent, "seq", 2 * k))
    return terms


def wide_gradients(normed, d_gu, cotangents, hidden):
    rows, width = normed.shape
    tile = 256
    first, second = d_gu.shape[1] // tile, hidden.shape[1] // tile

    def kernel(n_ref, dgu_ref, c_ref, h_ref, out_ref, left_ref):
        t = pl.program_id(0)

        @pl.when(t == 0)
        def _():
            left_ref[...] = n_ref[...].T

        @pl.when(t == first)
        def _():
            left_ref[...] = c_ref[...].T

        right = jnp.where(t < first, dgu_ref[...], h_ref[...])
        out_ref[...] = nn(left_ref[...], right).astype(BF16)

    return pl.pallas_call(
        kernel,
        grid=(first + second,),
        in_specs=[
            pl.BlockSpec((rows, width), lambda t: (0, 0)),
            pl.BlockSpec((rows, tile), lambda t: (0, jnp.minimum(t, first - 1))),
            pl.BlockSpec((rows, width), lambda t: (0, 0)),
            pl.BlockSpec((rows, tile), lambda t: (0, jnp.maximum(t - first, 0))),
        ],
        out_specs=pl.BlockSpec((width, tile), lambda t: (0, t)),
        out_shape=jax.ShapeDtypeStruct((width, (first + second) * tile), BF16),
        scratch_shapes=[pltpu.VMEM((width, rows), BF16)],
        compiler_params=params(1),
        cost_estimate=cost(20),
    )(normed, d_gu, cotangents, hidden)


def feed_forward(normed, d_hidden, gate_up):
    rows, width = normed.shape
    units = gate_up.shape[1] // 2
    tile = 256
    steps = units // tile

    def kernel(n_ref, dh_ref, g_ref, u_ref, hidden_ref, dgu_ref, dn_ref, acc_ref):
        t = pl.program_id(0)
        gate = nn(n_ref[...], g_ref[...])
        upper = nn(n_ref[...], u_ref[...])
        sigma = jax.nn.sigmoid(gate)
        silu = gate * sigma
        hidden_ref[...] = (silu * upper).astype(BF16)
        d_hid = dh_ref[...].astype(F32)
        d_gate = (d_hid * upper * (sigma * (1.0 + gate * (1.0 - sigma)))).astype(BF16)
        d_upper = (d_hid * silu).astype(BF16)
        at = pl.multiple_of(t * tile, tile)
        dgu_ref[:, pl.ds(at, tile)] = d_gate
        dgu_ref[:, pl.ds(units + at, tile)] = d_upper
        part = nt(d_gate, g_ref[...]) + nt(d_upper, u_ref[...])

        @pl.when(t == 0)
        def _():
            acc_ref[...] = part

        @pl.when(t > 0)
        def _():
            acc_ref[...] += part

        @pl.when(t == steps - 1)
        def _():
            dn_ref[...] = acc_ref[...].astype(BF16)

    return pl.pallas_call(
        kernel,
        grid=(steps,),
        in_specs=[
            pl.BlockSpec((rows, width), lambda t: (0, 0)),
            pl.BlockSpec((rows, tile), lambda t: (0, t)),
            pl.BlockSpec((width, tile), lambda t: (0, t)),
            pl.BlockSpec((width, tile), lambda t: (0, t + steps)),
        ],
        out_specs=[
            pl.BlockSpec((rows, tile), lambda t: (0, t)),
            pl.BlockSpec((rows, 2 * units), lambda t: (0, 0)),
            pl.BlockSpec((rows, width), lambda t: (0, 0)),
        ],
        out_shape=[
            jax.ShapeDtypeStruct((rows, units), BF16),
            jax.ShapeDtypeStruct((rows, 2 * units), BF16),
            jax.ShapeDtypeStruct((rows, width), BF16),
        ],
        scratch_shapes=[pltpu.VMEM((rows, width), F32)],
        compiler_params=params(1),
        cost_estimate=cost(29),
    )(normed, d_hidden, gate_up, gate_up)


def masks(doc_q, doc_k, stretch):
    keys = stretch + WIN
    row = lax.broadcasted_iota(jnp.int32, (keys, stretch), 0)
    place = jnp.where(row < stretch, row, row - keys)
    gap = lax.broadcasted_iota(jnp.int32, (keys, stretch), 1) - place
    same = doc_k == doc_q
    near = same & (gap >= 0) & (gap < WIN)
    far = same & (gap >= WIN)
    return near, far


def soft_pair(projected):
    one = jnp.exp(projected - jnp.max(projected, axis=0, keepdims=True))
    two = jnp.exp(jnp.min(projected, axis=0, keepdims=True) - projected)
    one = one * (1.0 / jnp.sum(one, axis=0, keepdims=True))
    two = two * (1.0 / jnp.sum(two, axis=0, keepdims=True))
    return jnp.concatenate([one, two], axis=0).astype(BF16)


def soft_pair_back(feat, grad):
    s1, s2 = feat[:HEAD_SIZE].astype(F32), feat[HEAD_SIZE:].astype(F32)
    t1, t2 = s1 * grad[:HEAD_SIZE], s2 * grad[HEAD_SIZE:]
    return (t1 - s1 * jnp.sum(t1, axis=0, keepdims=True)) - (
        t2 - s2 * jnp.sum(t2, axis=0, keepdims=True)
    )


def with_ones(value):
    tail = lax.broadcasted_iota(jnp.int32, (AUG - HEAD_SIZE, value.shape[1]), 0) == 0
    return jnp.concatenate([value, tail.astype(F32).astype(BF16)], axis=0)


def head_rows(h, size=HEAD_SIZE):
    return slice(h * size, (h + 1) * size)


def features_kernel(heads, groups, qkv_ref, halo_ref, maps_ref, keep_ref, fq_ref, fk_ref, state_ref):
    per = heads // groups
    base = heads * HEAD_SIZE
    keep = keep_ref[0].astype(BF16)
    for g in range(groups):
        rows = slice(base + g * HEAD_SIZE, base + (g + 1) * HEAD_SIZE)
        key = jnp.concatenate([qkv_ref[rows, :], halo_ref[0, head_rows(g), :]], axis=1)
        rows = slice(base + (groups + g) * HEAD_SIZE, base + (groups + g + 1) * HEAD_SIZE)
        value = jnp.concatenate([qkv_ref[rows, :], halo_ref[0, head_rows(groups + g), :]], axis=1)
        value = with_ones(value) * keep
        key_twice = jnp.concatenate([key, key], axis=0)
        for h in range(g * per, (g + 1) * per):
            query = qkv_ref[head_rows(h), :]
            fq_ref[0, head_rows(h, 128), :] = soft_pair(
                nn(maps_ref[0, h], jnp.concatenate([query, query], axis=0))
            )
            feat = soft_pair(nn(maps_ref[1, h], key_twice))
            fk_ref[0, head_rows(h, 128), :] = feat
            state_ref[0, head_rows(h, AUG), :] = nt(value, feat)


def attend_kernel(
    heads,
    groups,
    stretch,
    qkv_ref,
    halo_ref,
    fq_ref,
    fk_ref,
    prior_ref,
    docq_ref,
    dock_ref,
    use_ref,
    attn_ref,
    exact_ref,
    rden_ref,
    weight_ref,
):
    per = heads // groups
    base = heads * HEAD_SIZE
    near, far = masks(docq_ref[0], dock_ref[0], stretch)
    use = use_ref[0]
    for g in range(groups):
        rows = slice(base + g * HEAD_SIZE, base + (g + 1) * HEAD_SIZE)
        key = jnp.concatenate([qkv_ref[rows, :], halo_ref[0, head_rows(g), :]], axis=1)
        rows = slice(base + (groups + g) * HEAD_SIZE, base + (groups + g + 1) * HEAD_SIZE)
        value = jnp.concatenate([qkv_ref[rows, :], halo_ref[0, head_rows(groups + g), :]], axis=1)
        for h in range(g * per, (g + 1) * per):
            query = qkv_ref[head_rows(h), :]
            feat_q = fq_ref[0, head_rows(h, 128), :]
            scores = tn(key, query) * HEAD_SIZE ** (-0.5)
            linear = tn(fk_ref[0, head_rows(h, 128), :], feat_q)
            weight = jnp.where(near, jnp.exp(scores), jnp.where(far, linear, 0.0))
            narrow = weight.astype(BF16)
            weight_ref[0, h] = narrow
            before = nn(prior_ref[0, head_rows(h, AUG), :], feat_q) * use
            total = jnp.sum(weight, axis=0, keepdims=True) + before[HEAD_SIZE : HEAD_SIZE + 1]
            inverse = 1.0 / total
            exact = (nn(value, narrow) + before[:HEAD_SIZE]) * inverse
            exact_ref[0, head_rows(h), :] = exact
            attn_ref[head_rows(h), :] = exact.astype(BF16)
            rden_ref[0, h : h + 1, :] = inverse


def attend_back_kernel(
    heads,
    groups,
    stretch,
    qkv_ref,
    halo_ref,
    fq_ref,
    fk_ref,
    prior_ref,
    docq_ref,
    dock_ref,
    use_ref,
    exact_ref,
    rden_ref,
    weight_ref,
    dattn_ref,
    maps_ref,
    dq_ref,
    dkv_ref,
    dfk_ref,
    dprior_ref,
    dmaps_ref,
):
    per = heads // groups
    base = heads * HEAD_SIZE
    near, far = masks(docq_ref[0], dock_ref[0], stretch)
    use = use_ref[0]
    first_row = lax.broadcasted_iota(jnp.int32, (AUG - HEAD_SIZE, stretch), 0) == 0
    for g in range(groups):
        rows = slice(base + g * HEAD_SIZE, base + (g + 1) * HEAD_SIZE)
        key = jnp.concatenate([qkv_ref[rows, :], halo_ref[0, head_rows(g), :]], axis=1)
        rows = slice(base + (groups + g) * HEAD_SIZE, base + (groups + g + 1) * HEAD_SIZE)
        value = jnp.concatenate([qkv_ref[rows, :], halo_ref[0, head_rows(groups + g), :]], axis=1)
        d_key = jnp.zeros((HEAD_SIZE, stretch + WIN), F32)
        d_value = jnp.zeros((HEAD_SIZE, stretch + WIN), F32)
        for h in range(g * per, (g + 1) * per):
            query = qkv_ref[head_rows(h), :]
            feat_q = fq_ref[0, head_rows(h, 128), :]
            feat_k = fk_ref[0, head_rows(h, 128), :]
            weight = weight_ref[0, h]
            grad = dattn_ref[head_rows(h), :].astype(F32) * rden_ref[0, h : h + 1, :]
            lean = -jnp.sum(grad * exact_ref[0, head_rows(h), :], axis=0, keepdims=True)
            narrow = grad.astype(BF16)
            d_weight = tn(value, narrow) + lean
            d_score = jnp.where(near, d_weight * weight.astype(F32), 0.0).astype(BF16)
            d_linear = jnp.where(far, d_weight, 0.0).astype(BF16)
            both = jnp.concatenate([grad, jnp.where(first_row, lean, 0.0)], axis=0) * use
            both = both.astype(BF16)
            prior = prior_ref[0, head_rows(h, AUG), :]
            dprior_ref[0, head_rows(h, AUG), :] = nt(both, feat_q)
            d_feat = nn(feat_k, d_linear) + tn(prior, both)
            d_proj = soft_pair_back(feat_q, d_feat).astype(BF16)
            d_query = nn(key, d_score) * HEAD_SIZE ** (-0.5) + nn(maps_ref[0, h], d_proj)
            dq_ref[head_rows(h), :] = d_query.astype(BF16)
            dmaps_ref[0, h] = nt(query, d_proj)
            d_key += nt(query, d_score) * HEAD_SIZE ** (-0.5)
            d_value += nt(narrow, weight)
            dfk_ref[0, head_rows(h, 128), :] = nt(feat_q, d_linear).astype(BF16)
        dkv_ref[0, head_rows(g), :] = d_key
        dkv_ref[0, head_rows(groups + g), :] = d_value


def key_back_kernel(
    heads,
    groups,
    qkv_ref,
    halo_ref,
    fk_ref,
    keep_ref,
    dkv_ref,
    dfk_ref,
    dstate_ref,
    maps_ref,
    out_ref,
    dmaps_ref,
):
    per = heads // groups
    base = heads * HEAD_SIZE
    keep = keep_ref[0]
    keep_b = keep.astype(BF16)
    for g in range(groups):
        rows = slice(base + g * HEAD_SIZE, base + (g + 1) * HEAD_SIZE)
        key = jnp.concatenate([qkv_ref[rows, :], halo_ref[0, head_rows(g), :]], axis=1)
        rows = slice(base + (groups + g) * HEAD_SIZE, base + (groups + g + 1) * HEAD_SIZE)
        value = jnp.concatenate([qkv_ref[rows, :], halo_ref[0, head_rows(groups + g), :]], axis=1)
        value = with_ones(value) * keep_b
        d_key = dkv_ref[0, head_rows(g), :]
        d_value = dkv_ref[0, head_rows(groups + g), :]
        for h in range(g * per, (g + 1) * per):
            feat = fk_ref[0, head_rows(h, 128), :]
            d_state = dstate_ref[0, head_rows(h, AUG), :]
            d_feat = dfk_ref[0, head_rows(h, 128), :].astype(F32) + tn(d_state, value)
            d_value += nn(d_state[:HEAD_SIZE], feat) * keep
            d_proj = soft_pair_back(feat, d_feat).astype(BF16)
            d_key += nn(maps_ref[1, h], d_proj)
            dmaps_ref[0, h] = nt(key, d_proj)
        out_ref[0, head_rows(g), :] = d_key
        out_ref[0, head_rows(groups + g), :] = d_value


def lead(*shape):
    rest = (0,) * (len(shape))
    return pl.BlockSpec((1,) + shape, lambda b: (b,) + rest)


def cols(rows, width):
    return pl.BlockSpec((rows, width), lambda b: (0, b))


def fixed(*shape):
    rest = (0,) * len(shape)
    return pl.BlockSpec(shape, lambda b: rest)


def doc_of(starts, positions):
    return jnp.sum((starts[:, None, :] <= positions[None, :, None]).astype(jnp.int32), axis=2) - 1


def per_device(
    activations,
    cotangent,
    document_starts,
    norm_gain_pair,
    query_projection_weight,
    key_value_weight,
    output_projection_weight,
    gate_up_weight,
    down_weight,
    adapter_down_maps,
    query_adapter_up,
    keyval_adapter_up,
    output_adapter_down,
    output_adapter_up,
    hedgehog_maps,
):
    n_seq, n_kv = lax.axis_size("seq"), lax.axis_size("kv")
    me, level = lax.axis_index("seq"), lax.axis_index("kv")
    stretch = activations.shape[1]
    q_cols = query_projection_weight.shape[1]
    kv_cols = key_value_weight.shape[2]
    heads, groups = q_cols // HEAD_SIZE, kv_cols // HEAD_SIZE
    hidden_units = down_weight.shape[0]
    qkv_cols = q_cols + 2 * kv_cols
    keys = stretch + WIN
    share_rows = stretch // n_kv
    shard = norm_gain_pair.shape[1]
    begin = me * stretch
    rank = ADAPTER_RANK

    pack_a = jnp.concatenate(
        [
            query_projection_weight,
            key_value_weight[0],
            key_value_weight[1],
            jnp.pad(
                jnp.concatenate([adapter_down_maps, norm_gain_pair.T], axis=1),
                ((0, 0), (0, 128 - 3 * rank - 2)),
            ),
        ],
        axis=1,
    )
    pack_b = jnp.concatenate(
        [
            output_projection_weight.T,
            jnp.pad(output_adapter_up.T, ((0, 0), (0, 128 - rank))),
        ],
        axis=1,
    )
    pack_c = jnp.concatenate([gate_up_weight[0], gate_up_weight[1]], axis=1)
    by_hops = shard % 128 == 0
    if by_hops:
        pieces_a = second_hops(first_hops(pack_a))
        *pieces_a, pack_b, pack_c, pack_d = together(*pieces_a, pack_b, pack_c, down_weight.T)
        hops_b = first_hops(pack_b)
        full_a = ordered_rows(pieces_a)
    else:
        pack_d = down_weight.T
        full_a = lax.all_gather(pack_a, "seq", axis=0, tiled=True)
    full_d = lax.all_gather(pack_d, "seq", axis=0, tiled=True)
    full_c = lax.all_gather(pack_c, "seq", axis=0, tiled=True)
    gains = full_a[:, qkv_cols + 3 * rank : qkv_cols + 3 * rank + 2].T.astype(F32)
    up_rows = jnp.concatenate(
        [
            jnp.pad(query_adapter_up, ((0, 0), (0, 2 * kv_cols))),
            jnp.pad(keyval_adapter_up[0], ((0, 0), (q_cols, kv_cols))),
            jnp.pad(keyval_adapter_up[1], ((0, 0), (q_cols + kv_cols, 0))),
        ],
        axis=0,
    )

    maps_high = hedgehog_maps.astype(BF16)
    maps_rest = (hedgehog_maps - maps_high.astype(F32)).astype(BF16)
    maps_t = jnp.concatenate(
        [jnp.swapaxes(maps_high, 2, 3), jnp.swapaxes(maps_rest, 2, 3)], axis=3
    )

    pos_q = begin + jnp.arange(stretch, dtype=jnp.int32)
    pos_k = jnp.concatenate([pos_q, begin - WIN + jnp.arange(WIN, dtype=jnp.int32)])
    doc_q = doc_of(document_starts, pos_q)
    doc_k = doc_of(document_starts, pos_k)
    ends = (jnp.arange(-1, n_seq, dtype=jnp.int32) + 1) * stretch - WIN - 1
    doc_ends = doc_of(document_starts, ends)

    def doc_end(k):
        return lax.dynamic_index_in_dim(doc_ends, k + 1, axis=1, keepdims=False)

    doc_prev, doc_last = doc_end(me - 1), doc_end(me)
    keep = (doc_k == doc_last[:, None]) & (pos_k < begin + stretch - WIN)[None, :]
    keep = keep.astype(F32)[:, None, :]
    use = (doc_q == doc_prev[:, None]).astype(F32)[:, None, :]
    doc_q3, doc_k3 = doc_q[:, None, :], doc_k[:, :, None]

    def prefix(value, first):
        m = value.shape[0]
        total, found = value, jnp.zeros_like(value)
        bit = 1
        while bit < n_seq:
            other = flip(total.astype(BF16), "seq", bit).astype(F32)
            upper = (me & bit) != 0
            low_end = (me & ~(2 * bit - 1)) + bit - 1
            low_doc = doc_end(low_end)[first : first + m]
            join = (low_doc == doc_end(low_end + bit)[first : first + m])[:, None, None]
            wanted = ((low_doc == doc_prev[first : first + m]) & upper)[:, None, None]
            found = found + jnp.where(wanted, other, 0.0)
            below, above = jnp.where(upper, other, total), jnp.where(upper, total, other)
            total = above + jnp.where(join, below, 0.0)
            bit *= 2
        return found.astype(BF16)

    def suffix(value, first):
        m = value.shape[0]
        total, found = value, jnp.zeros_like(value)
        bit = 1
        while bit < n_seq:
            other = flip(total.astype(BF16), "seq", bit).astype(F32)
            upper = (me & bit) != 0
            low_first = me & ~(2 * bit - 1)
            high_doc = doc_end(low_first + bit - 1)[first : first + m]
            join = (high_doc == doc_end(low_first - 1)[first : first + m])[:, None, None]
            wanted = ((high_doc == doc_last[first : first + m]) & ~upper)[:, None, None]
            found = found + jnp.where(wanted, other, 0.0)
            below, above = jnp.where(upper, other, total), jnp.where(upper, total, other)
            total = below + jnp.where(join, above, 0.0)
            bit *= 2
        return found.astype(BF16)

    rows_all = MB * stretch
    inputs = activations.reshape(rows_all, MODEL_WIDTH)
    cotangents = cotangent.reshape(rows_all, MODEL_WIDTH)
    inputs_wide = inputs.astype(F32)
    scale_one = lax.rsqrt(jnp.mean(inputs_wide * inputs_wide, axis=1, keepdims=True) + EPSILON)
    normed_one = (inputs_wide * scale_one * gains[0:1]).astype(BF16)

    def own_rows(values):
        chunked = values.reshape(MB, n_kv, share_rows, values.shape[1])
        return lax.dynamic_index_in_dim(chunked, level, axis=1, keepdims=False)

    def by_level(values):
        return values.reshape(MB, n_kv, share_rows, MODEL_WIDTH)

    def padded(rows):
        return jnp.pad(rows, ((0, 128 - rows.shape[0]), (0, 0)))

    whole = tn(full_a, normed_one.T)
    adapt = whole[qkv_cols : qkv_cols + 3 * rank].astype(BF16)
    qkv = (whole[:qkv_cols] + tn(up_rows, adapt)).astype(BF16)
    edge = jnp.stack([qkv[q_cols:, (b + 1) * stretch - WIN : (b + 1) * stretch] for b in range(MB)])
    halo = shift(edge, "seq", 1)
    if by_hops:
        halo, *hops_b = together(halo, *hops_b)
        pieces_b = second_hops(hops_b)
    fq, fk, state = pl.pallas_call(
        functools.partial(features_kernel, heads, groups),
        grid=(MB,),
        in_specs=[
            cols(qkv_cols, stretch),
            lead(2 * kv_cols, WIN),
            fixed(2, heads, HEAD_SIZE, 2 * HEAD_SIZE),
            lead(1, keys),
        ],
        out_specs=[lead(heads * 128, stretch), lead(heads * 128, keys), lead(heads * AUG, 128)],
        out_shape=[
            jax.ShapeDtypeStruct((MB, heads * 128, stretch), BF16),
            jax.ShapeDtypeStruct((MB, heads * 128, keys), BF16),
            jax.ShapeDtypeStruct((MB, heads * AUG, 128), F32),
        ],
        compiler_params=params(1),
        cost_estimate=cost(5),
    )(qkv, halo, maps_t, keep)
    prior = prefix(state, 0)
    if by_hops:
        full_b = ordered_rows(pieces_b)
        full_b, prior = together(full_b, prior)
    else:
        full_b = lax.all_gather(pack_b, "seq", axis=0, tiled=True)
    attn, exact, rden, weight = pl.pallas_call(
        functools.partial(attend_kernel, heads, groups, stretch),
        grid=(MB,),
        in_specs=[
            cols(qkv_cols, stretch),
            lead(2 * kv_cols, WIN),
            lead(heads * 128, stretch),
            lead(heads * 128, keys),
            lead(heads * AUG, 128),
            lead(1, stretch),
            lead(keys, 1),
            lead(1, stretch),
        ],
        out_specs=[
            cols(q_cols, stretch),
            lead(q_cols, stretch),
            lead(heads, stretch),
            lead(heads, keys, stretch),
        ],
        out_shape=[
            jax.ShapeDtypeStruct((q_cols, rows_all), BF16),
            jax.ShapeDtypeStruct((MB, q_cols, stretch), F32),
            jax.ShapeDtypeStruct((MB, heads, stretch), F32),
            jax.ShapeDtypeStruct((MB, heads, keys, stretch), BF16),
        ],
        compiler_params=params(1),
        cost_estimate=cost(7),
    )(qkv, halo, fq, fk, prior, doc_q3, doc_k3, use)
    reduced = tn(output_adapter_down, attn)
    attn_aug = jnp.concatenate([attn, padded(reduced.astype(BF16))], axis=0)
    project = nt(attn_aug.T, full_b).astype(BF16)
    terms = level_send(by_level(project), 1)
    d_hidden = nn(cotangents, full_d).astype(BF16)
    x_own, c_own = own_rows(inputs), own_rows(cotangents)
    *terms, d_hidden, x_own, c_own = together(*terms, d_hidden, x_own, c_own)
    resid = x_own.astype(F32) + total_of(terms)
    pieces = level_spread(resid.astype(BF16))
    resid_all, normed_two = level_rows(pieces, BF16, gains[1:2])

    def weight_gradient(left, right, right_axis):
        return contract(left, right, ((0,), (right_axis,))).astype(BF16)

    def over_seq(part):
        return lax.psum_scatter(part, "seq", scatter_dimension=0, tiled=True)

    hidden, d_gu, d_normed = feed_forward(normed_two, d_hidden, full_c)
    terms = level_send(by_level(d_normed), 1)
    part_cd = wide_gradients(normed_two, d_gu, cotangents, hidden)
    core = me % 2
    first_one, second_one = parity_rows(normed_one, 1 - core), parity_rows(normed_one, core)
    *terms, part_cd, reduced, first_one, second_one = together(
        *terms, part_cd, reduced, first_one, second_one
    )
    grad_cd = over_seq(part_cd)
    d_normed = total_of(terms)
    scale = lax.rsqrt(jnp.mean(resid * resid, axis=2, keepdims=True) + EPSILON)
    gain_two = jnp.sum(d_normed * resid * scale, axis=(0, 1))
    weighted = gains[1] * d_normed
    d_resid = (
        c_own.astype(F32)
        + scale * weighted
        - resid * scale**3 * jnp.mean(weighted * resid, axis=2, keepdims=True)
    )
    pieces = level_spread(d_resid.astype(BF16))
    share = MODEL_WIDTH // n_kv
    down = nt(hidden, full_d).astype(BF16)
    reduce_all = sum_once(reduced, "kv").astype(BF16)
    *pieces, down, reduce_all = together(*pieces, down, reduce_all)
    d_branch = level_rows(pieces, BF16)

    back = tn(full_b, d_branch.T)
    d_reduce = back[q_cols : q_cols + rank].astype(BF16)
    d_attn = (back[:q_cols] + nn(output_adapter_down, d_reduce)).astype(BF16)
    d_attn, down = together(d_attn, down)
    down_terms = level_send(jnp.swapaxes(down.reshape(rows_all, n_kv, share), 0, 1), 0)
    d_query, d_kv, d_fk, d_prior, d_maps_q = pl.pallas_call(
        functools.partial(attend_back_kernel, heads, groups, stretch),
        grid=(MB,),
        in_specs=[
            cols(qkv_cols, stretch),
            lead(2 * kv_cols, WIN),
            lead(heads * 128, stretch),
            lead(heads * 128, keys),
            lead(heads * AUG, 128),
            lead(1, stretch),
            lead(keys, 1),
            lead(1, stretch),
            lead(q_cols, stretch),
            lead(heads, stretch),
            lead(heads, keys, stretch),
            cols(q_cols, stretch),
            fixed(2, heads, HEAD_SIZE, HEAD_SIZE),
        ],
        out_specs=[
            cols(q_cols, stretch),
            lead(2 * kv_cols, keys),
            lead(heads * 128, keys),
            lead(heads * AUG, 128),
            lead(heads, HEAD_SIZE, HEAD_SIZE),
        ],
        out_shape=[
            jax.ShapeDtypeStruct((q_cols, rows_all), BF16),
            jax.ShapeDtypeStruct((MB, 2 * kv_cols, keys), F32),
            jax.ShapeDtypeStruct((MB, heads * 128, keys), BF16),
            jax.ShapeDtypeStruct((MB, heads * AUG, 128), F32),
            jax.ShapeDtypeStruct((MB, heads, HEAD_SIZE, HEAD_SIZE), F32),
        ],
        compiler_params=params(1),
        cost_estimate=cost(13),
    )(
        qkv,
        halo,
        fq,
        fk,
        prior,
        doc_q3,
        doc_k3,
        use,
        exact,
        rden,
        weight,
        d_attn,
        maps_high,
    )
    d_state = suffix(d_prior, 0)
    right_b = jnp.concatenate([attn, padded(reduce_all)], axis=0)
    arrived_b = flip(weight_gradient(parity_rows(d_branch, 1 - core), right_b, 1), "seq", 1)
    kept_b = weight_gradient(parity_rows(d_branch, core), right_b, 1)
    d_state, kept_b = together(d_state, kept_b)
    d_kv, d_maps_k = pl.pallas_call(
        functools.partial(key_back_kernel, heads, groups),
        grid=(MB,),
        in_specs=[
            cols(qkv_cols, stretch),
            lead(2 * kv_cols, WIN),
            lead(heads * 128, keys),
            lead(1, keys),
            lead(2 * kv_cols, keys),
            lead(heads * 128, keys),
            lead(heads * AUG, 128),
            fixed(2, heads, HEAD_SIZE, HEAD_SIZE),
        ],
        out_specs=[lead(2 * kv_cols, keys), lead(heads, HEAD_SIZE, HEAD_SIZE)],
        out_shape=[
            jax.ShapeDtypeStruct((MB, 2 * kv_cols, keys), F32),
            jax.ShapeDtypeStruct((MB, heads, HEAD_SIZE, HEAD_SIZE), F32),
        ],
        compiler_params=params(1),
        cost_estimate=cost(7),
    )(qkv, halo, fk, keep, d_kv, d_fk, d_state, maps_high)
    d_kv, arrived_b, *down_terms = together(d_kv, arrived_b, *down_terms)
    terms_b = chip_pair(kept_b, arrived_b)
    back_edge = shift(d_kv[:, :, stretch:].astype(BF16), "seq", -1).astype(F32)
    d_kv = d_kv[:, :, :stretch] + jnp.pad(back_edge, ((0, 0), (0, 0), (stretch - WIN, 0)))
    d_kv = jnp.concatenate([d_kv[b] for b in range(MB)], axis=1).astype(BF16)
    d_qkv = jnp.concatenate([d_query, d_kv], axis=0)
    d_adapt = nn(up_rows, d_qkv)
    d_qkv_aug = jnp.concatenate([d_qkv, padded(d_adapt.astype(BF16))], axis=0)
    d_normed = nt(d_qkv_aug.T, full_a).astype(BF16)
    block_out = total_of(down_terms) + lax.dynamic_slice_in_dim(
        resid_all, level * share, share, 1
    ).astype(F32)
    block_out = block_out.astype(BF16).reshape(MB, stretch, share)
    terms = level_send(by_level(d_normed), 1)
    d_adapt_all = sum_once(d_adapt, "kv").astype(BF16)
    right_a = jnp.concatenate([d_qkv, padded(d_adapt_all)], axis=0)
    arrived_a = flip(weight_gradient(first_one, right_a, 1), "seq", 1)
    kept_a = weight_gradient(second_one, right_a, 1)
    terms_a = chip_pair(kept_a, arrived_a)
    lora = nt(adapt, d_qkv)
    ready = together(*terms, lora, *terms_b)
    terms, lora, terms_b = ready[:n_kv], ready[n_kv], ready[n_kv + 1 :]
    d_normed = total_of(terms)
    x_own = x_own.astype(F32)
    scale = own_rows(scale_one)
    gain_one = jnp.sum(d_normed * x_own * scale, axis=(0, 1))
    weighted = gains[0] * d_normed
    d_input = (
        d_resid
        + scale * weighted
        - x_own * scale**3 * jnp.mean(weighted * x_own, axis=2, keepdims=True)
    )
    pieces = level_spread(d_input.astype(BF16))

    gain_rows = jnp.stack([gain_one, gain_two])
    grad_gains = scatter_lanes(sum_once(gain_rows, "kv"), "seq")

    grad_lora_q = lora[:rank, :q_cols]
    grad_lora_k = lora[rank : 2 * rank, q_cols : q_cols + kv_cols]
    grad_lora_v = lora[2 * rank :, q_cols + kv_cols :]
    grad_reduce = nt(d_reduce, attn)
    d_maps = jnp.stack([d_maps_q.sum(0), d_maps_k.sum(0)])
    small = [grad_lora_q, grad_lora_k, grad_lora_v, grad_reduce, d_maps]
    sizes = [part.size // 128 for part in small]
    packed = sum_all(jnp.concatenate([part.reshape(-1, 128) for part in small], axis=0), "seq")
    outs, at = [], 0
    for part, size in zip(small, sizes):
        outs.append(packed[at : at + size].reshape(part.shape))
        at += size
    grad_lora_q, grad_lora_k, grad_lora_v, grad_reduce, grad_maps = outs

    ready = together(*pieces, grad_gains, *terms_a)
    pieces, grad_gains, terms_a = ready[:n_kv], ready[n_kv], ready[n_kv + 1 :]
    grad_a, grad_b = total_of(terms_a), total_of(terms_b)
    grad_cd = grad_cd.astype(F32)
    grad_c, grad_d = grad_cd[:, : 2 * hidden_units], grad_cd[:, 2 * hidden_units :]
    grad_enter = grad_a[:, qkv_cols : qkv_cols + 3 * rank]
    grad_expand = grad_b[:, q_cols : q_cols + rank].T
    grad_input = level_rows(pieces, F32).reshape(MB, stretch, MODEL_WIDTH)

    return (
        block_out,
        grad_input,
        grad_gains,
        grad_a[:, :q_cols],
        jnp.stack([grad_a[:, q_cols : q_cols + kv_cols], grad_a[:, q_cols + kv_cols : qkv_cols]]),
        grad_b[:, :q_cols].T,
        jnp.stack([grad_c[:, :hidden_units], grad_c[:, hidden_units:]]),
        grad_d.T,
        grad_enter,
        grad_lora_q,
        jnp.stack([grad_lora_k, grad_lora_v]),
        grad_reduce.T,
        grad_expand,
        grad_maps,
    )


def solution(mesh):
    placed = (
        P(None, "seq", None),
        P(None, "seq", None),
        P(),
        P(None, "seq"),
        P("seq", "kv"),
        P(None, "seq", "kv"),
        P("kv", "seq"),
        P(None, "seq", "kv"),
        P("kv", "seq"),
        P("seq", None),
        P(None, "kv"),
        P(None, None, "kv"),
        P("kv", None),
        P(None, "seq"),
        P(None, "kv", None, None),
    )
    return jax.shard_map(
        per_device,
        mesh=mesh,
        in_specs=placed,
        out_specs=(
            P(None, "seq", "kv"),
            P(None, "seq", None),
            P(None, "seq"),
            P("seq", "kv"),
            P(None, "seq", "kv"),
            P("kv", "seq"),
            P(None, "seq", "kv"),
            P("kv", "seq"),
            P("seq", None),
            P(None, "kv"),
            P(None, None, "kv"),
            P("kv", None),
            P(None, "seq"),
            P(None, "kv", None, None),
        ),
        check_vma=False,
    )
```

time: 2120 us -> 645 us (0.30)
  waiting for transfers between devices: 1280 us -> 225 us
  matrix products: 296 us -> 51.4 us
  blocking collectives: 143 us -> 0 us
  other arithmetic: 193 us -> 56 us
  Pallas kernels: 0 us -> 109 us
  starting transfers between devices: 18.2 us -> 82.7 us
  local copies, waits for them, and re-layouts: 134 us -> 97.6 us
  loops' own time: 21.7 us -> 0 us
    reduce_scatter x16 -> x1, waiting for transfers between devices: 770 us -> 0.01 us  [over_seq(): return lax.psum_scatter(part, 'seq', scatter_dimension=0, tiled=True)]
    psum x4 -> x0, waiting for transfers between devices: 317 us -> none  [the longest x1 150 us: per_device(): d_normed_two = lax.psum(norm_two_part, 'kv')]
    dot_general x128 -> x16, matrix products: 296 us -> 51.4 us  [contract(): lax.dot_general(left, right, (dims, ((), ())), preferred_element_type=F32)]
    ppermute x8 -> x66, waiting for transfers between devices: 3.31 us -> 225 us  [the longest x64 225 us: flip(): return lax.ppermute(value, axis, [(i, i ^ bit) for i in range(count)])]
    all_gather x9 -> x2, waiting for transfers between devices: 118 us -> 0.01 us  [the longest x1 0.01 us: per_device(): full_d = lax.all_gather(pack_d, 'seq', axis=0, tiled=True)]
    pallas_call x0 -> x11, Pallas kernels: none -> 109 us  [the longest x1 29.5 us: feed_forward(): pl.pallas_call(kernel, grid=(steps,), in_specs=[pl.BlockSpec((rows, width...]
    select_n x64 -> x0, other arithmetic: 95.1 us -> none  [turn(): return jax.tree.map(lambda a, b: jnp.where(reached, a, b), new, before)]
    all_gather x7 -> x0, blocking collectives: 69 us -> none  [the longest x2 20.5 us: prefix(): lax.all_gather(part.astype(kind), axis)]
  transfers between devices with their start and end apart: 39 -> 69, of which waited for: 26 -> 27; matrix products, arithmetic and copies ran while one was open for 24% -> 28% of each run, Pallas kernels for 0% -> 12%
where the time goes in v1:
time: 645 us; the launch traced here: 637 us
  waiting for transfers between devices  225 us (35%)
  Pallas kernels  109 us (17%)
  local copies, waits for them, and re-layouts  97.6 us (15%)
  starting transfers between devices  82.7 us (13%)
  other arithmetic  56 us (9%)
  matrix products  51.4 us (8%)
  between operations  15.4 us (2%)
    ppermute x64, waiting for transfers between devices, flip(): return lax.ppermute(value, axis, [(i, i ^ bit) for i in range(count)])  225 us
    ppermute x64, starting transfers between devices, flip(): return lax.ppermute(value, axis, [(i, i ^ bit) for i in range(count)])  78.7 us
    dot_general x16, matrix products, contract(): lax.dot_general(left, right, (dims, ((), ())), preferred_element_type=F32)  51.4 us
    unnamed x164, local copies, waits for them, and re-layouts  31.5 us
    pallas_call x1, Pallas kernels, feed_forward(): pl.pallas_call(kernel, grid=(steps,), in_specs=[pl.BlockSpec((rows, width...  29.5 us
    pallas_call x1, Pallas kernels, wide_gradients(): pl.pallas_call(kernel, grid=(first + second,), in_specs=[pl.BlockSpec((ro...  27.5 us
    dynamic_slice x4, local copies, waits for them, and re-layouts, parity_rows(): lax.dynamic_index_in_dim(view, parity, 2, keepdims=False)  22.5 us
    pallas_call x1, Pallas kernels, per_device(): pl.pallas_call(functools.partial(attend_back_kernel, heads, groups, stret...  13.1 us
  transfers between devices with their start and end apart: 69, of which 27 were waited for; matrix products, arithmetic and copies ran while one was open for 28% of the time, Pallas kernels for 12%

profile of v1, /device:TPU:0, one launch (start us, length us, event | category | flops | bytes accessed | tf_op | source)
XLA Modules:
  0.0 637.1 jit_solution(5636519022704618055)
XLA Ops:
  16.9 8.7 %collective-permute-done.5.refs_6_ = bf16[256,896]{1,0:T(8,128)(2,1)} collective-permute-done((bf16[256,896]{1,0:T(8,128)(2,1)S(1)}, bf16[256,896]{1,0:T(8,128)(2,1)}, u32[]{:S(2)}, u32[]{:S(2)}) %collective-permute-start.5) | collective-permute-done | bytes 458784 | tf_op jit(solution)/shard_map/ppermute | solution.py:50
  25.6 9.0 %collective-permute-done.3.refs_4_ = bf16[256,896]{1,0:T(8,128)(2,1)} collective-permute-done((bf16[256,896]{1,0:T(8,128)(2,1)S(1)}, bf16[256,896]{1,0:T(8,128)(2,1)}, u32[]{:S(2)}, u32[]{:S(2)}) %collective-permute-start.3) | collective-permute-done | bytes 458784 | tf_op jit(solution)/shard_map/ppermute | solution.py:50
  45.1 4.5 shard_map.254
  70.8 5.4 shard_map.255
  84.4 14.2 %collective-permute-done.16 = bf16[2,640,128]{2,1,0:T(8,128)(2,1)S(1)} collective-permute-done((bf16[2,640,128]{2,1,0:T(8,128)(2,1)S(1)}, bf16[2,640,128]{2,1,0:T(8,128)(2,1)S(1)}, u32[]{:S(2)}, u32[]{:S(2)}) %collective-permute-start.16) | collective-permute-done | bytes 327712 | tf_op jit(solution)/shard_map/ppermute | solution.py:50
  103.1 5.1 reshape.468
  116.7 7.2 %shard_map.257 = (bf16[512,512]{1,0:T(8,128)(2,1)}, f32[2,512,256]{2,1,0:T(8,128)}, f32[2,8,256]{2,1,0:T(8,128)}, bf16[2,8,320,256]{3,2,1,0:T(8,128)(2,1)}) custom-call(bf16[768,512]{1,0:T(8,128)(2,1)} %copy-done.29, bf16[2,256,64]{2,1,0:T(8,128)(2,1)} %collective-permute-done.7.halo_ref, bf16[2,1024,256]{2,1,0:T(8,128)(2,1)} %get-tuple-element.111.fq_ref, ...), custom_call_target="tpu_custom_call" | custom-call | flops 7699999744 | bytes 1048576 | tf_op jit(solution)/shard_map/pallas_call | solution.py:681
  133.6 9.9 %fusion.2.dh_ref = bf16[512,2048]{1,0:T(8,128)(2,1)} fusion(bf16[2048,2048]{0,1:T(8,128)(2,1)} %all-gather.3.cloned.1.call-done, bf16[512,2048]{1,0:T(8,128)(2,1)} %bitcast.224), kind=kOutput, calls=%fused_computation.11 | convolution fusion | flops 4296015872 | bytes 12582912 | tf_op jit(solution)/shard_map/dot_general | solution.py:23
  146.2 31.0 %collective-permute-done.19 = bf16[2,64,2048]{2,1,0:T(8,128)(2,1)S(1)} collective-permute-done((bf16[2,64,2048]{2,1,0:T(8,128)(2,1)}, bf16[2,64,2048]{2,1,0:T(8,128)(2,1)S(1)}, u32[]{:S(2)}, u32[]{:S(2)}) %collective-permute-start.19) | collective-permute-done | bytes 524320 | tf_op jit(solution)/shard_map/ppermute | solution.py:50
  187.7 5.6 constant_dynamic-slice_fusion.17
  193.3 5.8 copy.263
  199.1 4.7 copy.262
  203.8 21.9 %collective-permute-done.22.refs_2_ = bf16[2,64,2048]{2,1,0:T(8,128)(2,1)} collective-permute-done((bf16[2,64,2048]{2,1,0:T(8,128)(2,1)}, bf16[2,64,2048]{2,1,0:T(8,128)(2,1)}, u32[]{:S(2)}, u32[]{:S(2)}) %collective-permute-start.22) | collective-permute-done | bytes 524320 | tf_op jit(solution)/shard_map/ppermute | solution.py:50
  229.7 29.5 %shard_map.259 = (bf16[512,2048]{1,0:T(8,128)(2,1)}, bf16[512,4096]{1,0:T(8,128)(2,1)}, bf16[512,2048]{1,0:T(8,128)(2,1)}) custom-call(bf16[512,2048]{1,0:T(8,128)(2,1)} %bitcast.235, bf16[512,2048]{1,0:T(8,128)(2,1)} %fusion.2.dh_ref, bf16[2048,4096]{1,0:T(8,128)(2,1)} %all-gather.5.cloned.1.call-done.g_ref.u_ref, ...), custom_call_target="tpu_custom_call" | custom-call | flops 31900000256 | bytes 1048576 | tf_op jit(solution)/shard_map/pallas_call | solution.py:261
  266.3 27.5 %shard_map.260 = bf16[2048,6144]{1,0:T(8,128)(2,1)} custom-call(bf16[512,2048]{1,0:T(8,128)(2,1)} %bitcast.236, bf16[512,4096]{1,0:T(8,128)(2,1)} %get-tuple-element.134.dgu_ref, bf16[512,2048]{1,0:T(8,128)(2,1)} %bitcast.225, bf16[512,2048]{1,0:T(8,128)(2,1)} %get-tuple-element.135.h_ref), custom_call_target="tpu_custom_call" | custom-call | flops 22000001024 | bytes 1048576 | tf_op jit(solution)/shard_map/pallas_call | solution.py:211
  293.8 13.0 %collective-permute-done.25 = bf16[2,64,2048]{2,1,0:T(8,128)(2,1)S(1)} collective-permute-done((bf16[2,64,2048]{2,1,0:T(8,128)(2,1)}, bf16[2,64,2048]{2,1,0:T(8,128)(2,1)S(1)}, u32[]{:S(2)}, u32[]{:S(2)}) %collective-permute-start.25) | collective-permute-done | bytes 524320 | tf_op jit(solution)/shard_map/ppermute | solution.py:50
  318.4 10.9 %convolution_convert_fusion.1 = bf16[512,2048]{1,0:T(8,128)(2,1)} fusion(bf16[512,2048]{1,0:T(8,128)(2,1)S(1)} %copy-done.72, bf16[2048,2048]{0,1:T(8,128)(2,1)} %all-gather.3.cloned.1.call-done), kind=kOutput, calls=%fused_computation.8 | convolution fusion | flops 4296015872 | bytes 12582912 | tf_op jit(solution)/shard_map/dot_general | solution.py:23
  330.7 26.8 %collective-permute-done.28.refs_2_ = bf16[2,64,2048]{2,1,0:T(8,128)(2,1)S(1)} collective-permute-done((bf16[2,64,2048]{2,1,0:T(8,128)(2,1)S(1)}, bf16[2,64,2048]{2,1,0:T(8,128)(2,1)S(1)}, u32[]{:S(2)}, u32[]{:S(2)}) %collective-permute-start.28) | collective-permute-done | bytes 524320 | tf_op jit(solution)/shard_map/ppermute | solution.py:50
  370.9 13.1 %shard_map.262 = (bf16[512,512]{1,0:T(8,128)(2,1)}, f32[2,256,320]{2,1,0:T(8,128)}, bf16[2,1024,320]{2,1,0:T(8,128)(2,1)}, f32[2,640,128]{2,1,0:T(8,128)}, f32[2,8,64,64]{3,2,1,0:T(8,128)}) custom-call(bf16[768,512]{1,0:T(8,128)(2,1)} %copy-done.29, bf16[2,256,64]{2,1,0:T(8,128)(2,1)} %collective-permute-done.7.halo_ref, ...), custom_call_target="tpu_custom_call" | custom-call | flops 14300000256 | bytes 1048576 | tf_op jit(solution)/shard_map/pallas_call | solution.py:756
  385.4 6.3 constant_dynamic-slice_fusion.13
  397.5 5.9 copy.303
  403.4 5.8 copy.302
  433.3 6.9 %shard_map.263 = (f32[2,256,320]{2,1,0:T(8,128)}, f32[2,8,64,64]{3,2,1,0:T(8,128)}) custom-call(bf16[768,512]{1,0:T(8,128)(2,1)} %copy-done.29, bf16[2,256,64]{2,1,0:T(8,128)(2,1)} %collective-permute-done.7.halo_ref, bf16[2,1024,320]{2,1,0:T(8,128)(2,1)} %get-tuple-element.110.fk_ref, f32[2,1,320]{2,1,0:T(1,128)} %and_convert_fusion.keep_ref, ...), custom_call_target="tpu_custom_call" | custom-call | flops 7699999744 | bytes 1048576 | tf_op jit(solution)/shard_map/pallas_call | solution.py:810
  446.5 14.8 %collective-permute-done.38 = bf16[512,512]{1,0:T(8,128)(2,1)} collective-permute-done((bf16[512,512]{1,0:T(8,128)(2,1)}, bf16[512,512]{1,0:T(8,128)(2,1)}, u32[]{:S(2)}, u32[]{:S(2)}) %collective-permute-start.38) | collective-permute-done | bytes 524320 | tf_op jit(solution)/shard_map/ppermute | solution.py:50
  476.6 11.0 %collective-permute-start.57 = (bf16[24,512]{1,0:T(8,128)(2,1)S(1)}, bf16[24,512]{1,0:T(8,128)(2,1)S(1)}, u32[]{:S(2)}, u32[]{:S(2)}) collective-permute-start(bf16[24,512]{1,0:T(8,128)(2,1)S(1)} %convolution_convert_fusion.7), channel_id=1, source_target_pairs={{0,2},{1,3},{2,0},{3,1},{4,6},{5,7},{6,4},{7,5},{8,10},{9,11},{10,... | collective-permute-start | bytes 73736 | tf_op jit(solution)/shard_map/ppermute | solution.py:50
  504.1 5.8 collective-permute-done.46
  510.6 31.3 %collective-permute-done.42 = bf16[2,64,2048]{2,1,0:T(8,128)(2,1)S(1)} collective-permute-done((bf16[2,64,2048]{2,1,0:T(8,128)(2,1)S(1)}, bf16[2,64,2048]{2,1,0:T(8,128)(2,1)S(1)}, u32[]{:S(2)}, u32[]{:S(2)}) %collective-permute-start.42) | collective-permute-done | bytes 524320 | tf_op jit(solution)/shard_map/ppermute | solution.py:50
  571.6 4.7 collective-permute-done.64
  578.3 5.2 collective-permute-done.65
  594.4 6.9 %collective-permute-done.48.refs_2_ = bf16[2,64,2048]{2,1,0:T(8,128)(2,1)S(1)} collective-permute-done((bf16[2,64,2048]{2,1,0:T(8,128)(2,1)}, bf16[2,64,2048]{2,1,0:T(8,128)(2,1)S(1)}, u32[]{:S(2)}, u32[]{:S(2)}) %collective-permute-start.48) | collective-permute-done | bytes 524320 | tf_op jit(solution)/shard_map/ppermute | solution.py:50
  601.5 9.1 %collective-permute-done.61 = bf16[256,896]{0,1:T(8,128)(2,1)} collective-permute-done((bf16[256,896]{0,1:T(8,128)(2,1)S(1)}, bf16[256,896]{0,1:T(8,128)(2,1)}, u32[]{:S(2)}, u32[]{:S(2)}) %collective-permute-start.61) | collective-permute-done | bytes 458784 | tf_op jit(solution)/shard_map/ppermute | solution.py:50
  625.5 4.7 pad_maximum_fusion
  (427 shorter events, 249.5 us)
Async XLA Ops:
  7.2 126.4 %all-gather.3.cloned.1.call-start = ((), (), s32[]{:S(2)}) async-start(), calls=%async_computation.1 | async-start | bytes 9437184 | tf_op jit(solution)/shard_map/all_gather | solution.py:564
  37.4 192.2 %all-gather.5.cloned.1.call-start = ((), (), s32[]{:S(2)}) async-start(), calls=%async_computation.2 | async-start | bytes 18874368 | tf_op jit(solution)/shard_map/all_gather | solution.py:565
  38.2 580.4 %reduce-scatter.2.cloned.1.call-start = ((), (), s32[]{:S(2)}) async-start(), calls=%async_computation.3 | async-start | bytes 28311552 | tf_op jit(solution)/shard_map/reduce_scatter | solution.py:724
  41.6 26.4 %collective-permute-start.10 = (bf16[256,640]{1,0:T(8,128)(2,1)S(1)}, bf16[256,640]{1,0:T(8,128)(2,1)}, u32[]{:S(2)}, u32[]{:S(2)}) collective-permute-start(bf16[256,640]{1,0:T(8,128)(2,1)S(1)} %fusion.55.refs_0_), channel_id=1, source_target_pairs={{0,24},{4,28},{8,16},{12,20},{16,8},{20,12},{24,0},{28,4},{1,25},{... | collective-permute-start | bytes 983048 | tf_op jit(solution)/shard_map/ppermute | solution.py:50
  43.5 24.6 %collective-permute-start.9 = (bf16[256,640]{1,0:T(8,128)(2,1)S(1)}, bf16[256,640]{1,0:T(8,128)(2,1)}, u32[]{:S(2)}, u32[]{:S(2)}) collective-permute-start(bf16[256,640]{1,0:T(8,128)(2,1)S(1)} %fusion.55.refs_0_), channel_id=1, source_target_pairs={{0,16},{4,20},{8,24},{12,28},{16,0},{20,4},{24,8},{28,12},{1,17},{... | collective-permute-start | bytes 983048 | tf_op jit(solution)/shard_map/ppermute | solution.py:50
  44.8 26.0 %collective-permute-start.8 = (bf16[256,640]{1,0:T(8,128)(2,1)S(1)}, bf16[256,640]{1,0:T(8,128)(2,1)}, u32[]{:S(2)}, u32[]{:S(2)}) collective-permute-start(bf16[256,640]{1,0:T(8,128)(2,1)S(1)} %fusion.55.refs_0_), channel_id=1, source_target_pairs={{0,8},{4,12},{8,0},{12,4},{16,24},{20,28},{24,16},{28,20},{1,9},{5... | collective-permute-start | bytes 983048 | tf_op jit(solution)/shard_map/ppermute | solution.py:50
  83.3 27.8 %collective-permute-start.11 = (bf16[256,640]{1,0:T(8,128)(2,1)}, bf16[256,640]{1,0:T(8,128)(2,1)}, u32[]{:S(2)}, u32[]{:S(2)}) collective-permute-start(bf16[256,640]{1,0:T(8,128)(2,1)} %copy-done.28), channel_id=1, source_target_pairs={{0,4},{4,0},{8,12},{12,8},{16,20},{20,16},{24,28},{28,24},{1,5},{5... | collective-permute-start | bytes 983048 | tf_op jit(solution)/shard_map/ppermute | solution.py:50
  83.4 27.7 %collective-permute-start.12 = (bf16[256,640]{1,0:T(8,128)(2,1)}, bf16[256,640]{1,0:T(8,128)(2,1)}, u32[]{:S(2)}, u32[]{:S(2)}) collective-permute-start(bf16[256,640]{1,0:T(8,128)(2,1)} %collective-permute-done.8.refs_2_), channel_id=1, source_target_pairs={{0,4},{4,0},{8,12},{12,8},{16,20},{20,16},{24,28},{28,24},{1,5},{5... | collective-permute-start | bytes 983048 | tf_op jit(solution)/shard_map/ppermute | solution.py:50
  83.9 27.3 %collective-permute-start.13 = (bf16[256,640]{1,0:T(8,128)(2,1)}, bf16[256,640]{1,0:T(8,128)(2,1)}, u32[]{:S(2)}, u32[]{:S(2)}) collective-permute-start(bf16[256,640]{1,0:T(8,128)(2,1)} %collective-permute-done.9.refs_4_), channel_id=1, source_target_pairs={{0,4},{4,0},{8,12},{12,8},{16,20},{20,16},{24,28},{28,24},{1,5},{5... | collective-permute-start | bytes 983048 | tf_op jit(solution)/shard_map/ppermute | solution.py:50
  84.0 27.2 %collective-permute-start.14 = (bf16[256,640]{1,0:T(8,128)(2,1)}, bf16[256,640]{1,0:T(8,128)(2,1)}, u32[]{:S(2)}, u32[]{:S(2)}) collective-permute-start(bf16[256,640]{1,0:T(8,128)(2,1)} %collective-permute-done.10.refs_6_), channel_id=1, source_target_pairs={{0,4},{4,0},{8,12},{12,8},{16,20},{20,16},{24,28},{28,24},{1,5},{5... | collective-permute-start | bytes 983048 | tf_op jit(solution)/shard_map/ppermute | solution.py:50
  132.8 44.4 %collective-permute-start.19 = (bf16[2,64,2048]{2,1,0:T(8,128)(2,1)}, bf16[2,64,2048]{2,1,0:T(8,128)(2,1)S(1)}, u32[]{:S(2)}, u32[]{:S(2)}) collective-permute-start(bf16[2,64,2048]{2,1,0:T(8,128)(2,1)} %get-tuple-element.308), channel_id=1, source_target_pairs={{0,2},{1,3},{2,0},{3,1},{4,6},{5,7},{6,4},{7,5},{8,10},{9,11},{10,... | collective-permute-start | bytes 1572872 | tf_op jit(solution)/shard_map/ppermute | solution.py:50
  132.8 44.4 %collective-permute-start.18 = (bf16[2,64,2048]{2,1,0:T(8,128)(2,1)S(1)}, bf16[2,64,2048]{2,1,0:T(8,128)(2,1)S(1)}, u32[]{:S(2)}, u32[]{:S(2)}) collective-permute-start(bf16[2,64,2048]{2,1,0:T(8,128)(2,1)S(1)} %get-tuple-element.309), channel_id=1, source_target_pairs={{0,1},{1,0},{2,3},{3,2},{4,5},{5,4},{6,7},{7,6},{8,9},{9,8},{10,11... | collective-permute-start | bytes 1572872 | tf_op jit(solution)/shard_map/ppermute | solution.py:50
  180.6 23.3 %collective-permute-start.23 = (bf16[2,64,2048]{2,1,0:T(8,128)(2,1)}, bf16[2,64,2048]{2,1,0:T(8,128)(2,1)}, u32[]{:S(2)}, u32[]{:S(2)}) collective-permute-start(bf16[2,64,2048]{2,1,0:T(8,128)(2,1)} %convert_element_type.406.refs_0_), channel_id=1, source_target_pairs={{0,3},{1,2},{2,1},{3,0},{4,7},{5,6},{6,5},{7,4},{8,11},{9,10},{10,... | collective-permute-start | bytes 1572872 | tf_op jit(solution)/shard_map/ppermute | solution.py:50
  182.9 42.8 %collective-permute-start.22 = (bf16[2,64,2048]{2,1,0:T(8,128)(2,1)}, bf16[2,64,2048]{2,1,0:T(8,128)(2,1)}, u32[]{:S(2)}, u32[]{:S(2)}) collective-permute-start(bf16[2,64,2048]{2,1,0:T(8,128)(2,1)} %convert_element_type.406.refs_0_), channel_id=1, source_target_pairs={{0,2},{1,3},{2,0},{3,1},{4,6},{5,7},{6,4},{7,5},{8,10},{9,11},{10,... | collective-permute-start | bytes 1572872 | tf_op jit(solution)/shard_map/ppermute | solution.py:50
  183.0 42.8 %collective-permute-start.21 = (bf16[2,64,2048]{2,1,0:T(8,128)(2,1)}, bf16[2,64,2048]{2,1,0:T(8,128)(2,1)}, u32[]{:S(2)}, u32[]{:S(2)}) collective-permute-start(bf16[2,64,2048]{2,1,0:T(8,128)(2,1)} %convert_element_type.406.refs_0_), channel_id=1, source_target_pairs={{0,1},{1,0},{2,3},{3,2},{4,5},{5,4},{6,7},{7,6},{8,9},{9,8},{10,11... | collective-permute-start | bytes 1572872 | tf_op jit(solution)/shard_map/ppermute | solution.py:50
  261.9 31.9 %collective-permute-start.26 = (bf16[2,64,2048]{2,1,0:T(8,128)(2,1)}, bf16[2,64,2048]{2,1,0:T(8,128)(2,1)S(1)}, u32[]{:S(2)}, u32[]{:S(2)}) collective-permute-start(bf16[2,64,2048]{2,1,0:T(8,128)(2,1)} %get-tuple-element.303), channel_id=1, source_target_pairs={{0,3},{1,2},{2,1},{3,0},{4,7},{5,6},{6,5},{7,4},{8,11},{9,10},{10,... | collective-permute-start | bytes 1572872 | tf_op jit(solution)/shard_map/ppermute | solution.py:50
  264.2 42.7 %collective-permute-start.25 = (bf16[2,64,2048]{2,1,0:T(8,128)(2,1)}, bf16[2,64,2048]{2,1,0:T(8,128)(2,1)S(1)}, u32[]{:S(2)}, u32[]{:S(2)}) collective-permute-start(bf16[2,64,2048]{2,1,0:T(8,128)(2,1)} %get-tuple-element.304), channel_id=1, source_target_pairs={{0,2},{1,3},{2,0},{3,1},{4,6},{5,7},{6,4},{7,5},{8,10},{9,11},{10,... | collective-permute-start | bytes 1572872 | tf_op jit(solution)/shard_map/ppermute | solution.py:50
  264.2 42.7 %collective-permute-start.24 = (bf16[2,64,2048]{2,1,0:T(8,128)(2,1)}, bf16[2,64,2048]{2,1,0:T(8,128)(2,1)S(1)}, u32[]{:S(2)}, u32[]{:S(2)}) collective-permute-start(bf16[2,64,2048]{2,1,0:T(8,128)(2,1)} %get-tuple-element.305), channel_id=1, source_target_pairs={{0,1},{1,0},{2,3},{3,2},{4,5},{5,4},{6,7},{7,6},{8,9},{9,8},{10,11... | collective-permute-start | bytes 1572872 | tf_op jit(solution)/shard_map/ppermute | solution.py:50
  315.1 42.4 %collective-permute-start.28 = (bf16[2,64,2048]{2,1,0:T(8,128)(2,1)S(1)}, bf16[2,64,2048]{2,1,0:T(8,128)(2,1)S(1)}, u32[]{:S(2)}, u32[]{:S(2)}) collective-permute-start(bf16[2,64,2048]{2,1,0:T(8,128)(2,1)S(1)} %fusion.100.refs_0_), channel_id=1, source_target_pairs={{0,2},{1,3},{2,0},{3,1},{4,6},{5,7},{6,4},{7,5},{8,10},{9,11},{10,... | collective-permute-start | bytes 1572872 | tf_op jit(solution)/shard_map/ppermute | solution.py:50
  315.1 42.4 %collective-permute-start.27 = (bf16[2,64,2048]{2,1,0:T(8,128)(2,1)S(1)}, bf16[2,64,2048]{2,1,0:T(8,128)(2,1)S(1)}, u32[]{:S(2)}, u32[]{:S(2)}) collective-permute-start(bf16[2,64,2048]{2,1,0:T(8,128)(2,1)S(1)} %fusion.100.refs_0_), channel_id=1, source_target_pairs={{0,1},{1,0},{2,3},{3,2},{4,5},{5,4},{6,7},{7,6},{8,9},{9,8},{10,11... | collective-permute-start | bytes 1572872 | tf_op jit(solution)/shard_map/ppermute | solution.py:50
  412.7 48.6 %collective-permute-start.36 = (bf16[1024,640]{1,0:T(8,128)(2,1)}, bf16[1024,640]{1,0:T(8,128)(2,1)}, u32[]{:S(2)}, u32[]{:S(2)}) collective-permute-start(bf16[1024,640]{1,0:T(8,128)(2,1)} %convolution_convert_fusion.5), channel_id=1, source_target_pairs={{0,4},{4,0},{8,12},{12,8},{16,20},{20,16},{24,28},{28,24},{1,5},{5... | collective-permute-start | bytes 3932168 | tf_op jit(solution)/shard_map/ppermute | solution.py:50
  422.7 23.8 %collective-permute-start.37 = (bf16[512,512]{1,0:T(8,128)(2,1)}, bf16[512,512]{1,0:T(8,128)(2,1)}, u32[]{:S(2)}, u32[]{:S(2)}) collective-permute-start(bf16[512,512]{1,0:T(8,128)(2,1)} %bitcast.189), channel_id=1, source_target_pairs={{0,1},{1,0},{2,3},{3,2},{4,5},{5,4},{6,7},{7,6},{8,9},{9,8},{10,11... | collective-permute-start | bytes 1572872 | tf_op jit(solution)/shard_map/ppermute | solution.py:50
  422.8 38.6 %collective-permute-start.38 = (bf16[512,512]{1,0:T(8,128)(2,1)}, bf16[512,512]{1,0:T(8,128)(2,1)}, u32[]{:S(2)}, u32[]{:S(2)}) collective-permute-start(bf16[512,512]{1,0:T(8,128)(2,1)} %bitcast.188), channel_id=1, source_target_pairs={{0,2},{1,3},{2,0},{3,1},{4,6},{5,7},{6,4},{7,5},{8,10},{9,11},{10,... | collective-permute-start | bytes 1572872 | tf_op jit(solution)/shard_map/ppermute | solution.py:50
  424.3 37.0 %collective-permute-start.39 = (bf16[512,512]{1,0:T(8,128)(2,1)}, bf16[512,512]{1,0:T(8,128)(2,1)}, u32[]{:S(2)}, u32[]{:S(2)}) collective-permute-start(bf16[512,512]{1,0:T(8,128)(2,1)} %bitcast.187), channel_id=1, source_target_pairs={{0,3},{1,2},{2,1},{3,0},{4,7},{5,6},{6,5},{7,4},{8,11},{9,10},{10,... | collective-permute-start | bytes 1572872 | tf_op jit(solution)/shard_map/ppermute | solution.py:50
  468.3 32.5 %collective-permute-start.44 = (bf16[256,640]{0,1:T(8,128)(2,1)}, bf16[256,640]{0,1:T(8,128)(2,1)}, u32[]{:S(2)}, u32[]{:S(2)}) collective-permute-start(bf16[256,640]{0,1:T(8,128)(2,1)} %bitcast.215), channel_id=1, source_target_pairs={{0,8},{4,12},{8,0},{12,4},{16,24},{20,28},{24,16},{28,20},{1,9},{5... | collective-permute-start | bytes 983048 | tf_op jit(solution)/shard_map/ppermute | solution.py:50
  469.4 34.8 %collective-permute-start.45 = (bf16[256,640]{0,1:T(8,128)(2,1)}, bf16[256,640]{0,1:T(8,128)(2,1)}, u32[]{:S(2)}, u32[]{:S(2)}) collective-permute-start(bf16[256,640]{0,1:T(8,128)(2,1)} %bitcast.213), channel_id=1, source_target_pairs={{0,16},{4,20},{8,24},{12,28},{16,0},{20,4},{24,8},{28,12},{1,17},{... | collective-permute-start | bytes 983048 | tf_op jit(solution)/shard_map/ppermute | solution.py:50
  495.3 46.6 %collective-permute-start.42 = (bf16[2,64,2048]{2,1,0:T(8,128)(2,1)S(1)}, bf16[2,64,2048]{2,1,0:T(8,128)(2,1)S(1)}, u32[]{:S(2)}, u32[]{:S(2)}) collective-permute-start(bf16[2,64,2048]{2,1,0:T(8,128)(2,1)S(1)} %get-tuple-element.292), channel_id=1, source_target_pairs={{0,2},{1,3},{2,0},{3,1},{4,6},{5,7},{6,4},{7,5},{8,10},{9,11},{10,... | collective-permute-start | bytes 1572872 | tf_op jit(solution)/shard_map/ppermute | solution.py:50
  497.3 44.5 %collective-permute-start.41 = (bf16[2,64,2048]{2,1,0:T(8,128)(2,1)S(1)}, bf16[2,64,2048]{2,1,0:T(8,128)(2,1)S(1)}, u32[]{:S(2)}, u32[]{:S(2)}) collective-permute-start(bf16[2,64,2048]{2,1,0:T(8,128)(2,1)S(1)} %get-tuple-element.293), channel_id=1, source_target_pairs={{0,1},{1,0},{2,3},{3,2},{4,5},{5,4},{6,7},{7,6},{8,9},{9,8},{10,11... | collective-permute-start | bytes 1572872 | tf_op jit(solution)/shard_map/ppermute | solution.py:50
  504.1 79.4 %collective-permute-start.59 = (bf16[1024,896]{1,0:T(8,128)(2,1)}, bf16[1024,896]{1,0:T(8,128)(2,1)}, u32[]{:S(2)}, u32[]{:S(2)}) collective-permute-start(bf16[1024,896]{1,0:T(8,128)(2,1)} %convolution_convert_fusion.4), channel_id=1, source_target_pairs={{0,4},{4,0},{8,12},{12,8},{16,20},{20,16},{24,28},{28,24},{1,5},{5... | collective-permute-start | bytes 5505032 | tf_op jit(solution)/shard_map/ppermute | solution.py:50
  556.2 33.6 %collective-permute-start.49 = (bf16[2,64,2048]{2,1,0:T(8,128)(2,1)}, bf16[2,64,2048]{2,1,0:T(8,128)(2,1)S(1)}, u32[]{:S(2)}, u32[]{:S(2)}) collective-permute-start(bf16[2,64,2048]{2,1,0:T(8,128)(2,1)} %fusion.11.refs_0_), channel_id=1, source_target_pairs={{0,3},{1,2},{2,1},{3,0},{4,7},{5,6},{6,5},{7,4},{8,11},{9,10},{10,... | collective-permute-start | bytes 1572872 | tf_op jit(solution)/shard_map/ppermute | solution.py:50
  557.6 43.7 %collective-permute-start.48 = (bf16[2,64,2048]{2,1,0:T(8,128)(2,1)}, bf16[2,64,2048]{2,1,0:T(8,128)(2,1)S(1)}, u32[]{:S(2)}, u32[]{:S(2)}) collective-permute-start(bf16[2,64,2048]{2,1,0:T(8,128)(2,1)} %fusion.11.refs_0_), channel_id=1, source_target_pairs={{0,2},{1,3},{2,0},{3,1},{4,6},{5,7},{6,4},{7,5},{8,10},{9,11},{10,... | collective-permute-start | bytes 1572872 | tf_op jit(solution)/shard_map/ppermute | solution.py:50
  557.6 43.7 %collective-permute-start.47 = (bf16[2,64,2048]{2,1,0:T(8,128)(2,1)}, bf16[2,64,2048]{2,1,0:T(8,128)(2,1)}, u32[]{:S(2)}, u32[]{:S(2)}) collective-permute-start(bf16[2,64,2048]{2,1,0:T(8,128)(2,1)} %fusion.11.refs_0_), channel_id=1, source_target_pairs={{0,1},{1,0},{2,3},{3,2},{4,5},{5,4},{6,7},{7,6},{8,9},{9,8},{10,11... | collective-permute-start | bytes 1572872 | tf_op jit(solution)/shard_map/ppermute | solution.py:50
  (110 other events, 1385.1 us)
Sparse Core Ops, SparseCore 0:
  37.5 72.8 all-gather.2
  112.3 89.8 all-gather.4
  307.0 161.3 reduce-scatter.1
